TPU v7x, 256 devices: a whole 4x4x8 slice. The times are simulated.
256 devices in a mesh: segment: 4 (over x), dom: 32 (over z, y), dp: 2 (over core).
Axes of the slice: x: 4, y: 4, z: 8, core: 2. Of those that a mesh axis runs over, the one named last changes fastest.
Arguments:
- node_in: bfloat16 [4, 4096, 512], P('dp', 'dom'), may hold values from -6 to 6
- edge_in: bfloat16 [4, 4096, 512], P('dp', 'dom'), may hold values from -6 to 6
- node_cot: bfloat16 [4, 4096, 512], P('dp', 'dom'), may hold values from -6 to 6
- edge_cot: bfloat16 [4, 4096, 512], P('dp', 'dom'), may hold values from -6 to 6
- send_rows: int32 [4096], P('dom'), may hold values from 0 to 127
- sender_row: int32 [4096], P('dom'), may hold values from 0 to 255
- receiver_row: int32 [4096], P('dom'), may hold values from 0 to 127
- edge_count: int32 [32], P('dom'), may hold values from 1 to 128, 3072 in all
- edge_w1: bfloat16 [4, 1536, 512], P('segment'), may hold values from -0.15625 to 0.15625
- edge_w2: bfloat16 [4, 512, 512], P('segment'), may hold values from -0.25 to 0.25
- node_w1: bfloat16 [4, 1024, 512], P('segment'), may hold values from -0.1875 to 0.1875
- node_w2: bfloat16 [4, 512, 512], P('segment'), may hold values from -0.25 to 0.25
- vectors: bfloat16 [4, 8, 512], P('segment'), may hold values from -2 to 2, as said below
Outputs:
- node_out: bfloat16 [4, 4, 4096, 512], P('segment', 'dp', 'dom')
- edge_out: bfloat16 [4, 4, 4096, 512], P('segment', 'dp', 'dom')
- node_grad: float32 [4, 4, 4096, 512], P('segment', 'dp', 'dom')
- edge_grad: float32 [4, 4, 4096, 512], P('segment', 'dp', 'dom')
- grad_edge_w1: float32 [4, 1536, 512], P('segment', None, ('dom', 'dp'))
- grad_edge_w2: float32 [4, 512, 512], P('segment', None, ('dom', 'dp'))
- grad_node_w1: float32 [4, 1024, 512], P('segment', None, ('dom', 'dp'))
- grad_node_w2: float32 [4, 512, 512], P('segment', None, ('dom', 'dp'))
- grad_vectors: float32 [4, 8, 512], P('segment', None, ('dom', 'dp'))
Inputs may be any that keep to these rules, and one draw needn't show every extreme that they name: `vectors`: the parameter rows 2 and 6 of each layer are norm gains between 0.5 and 1.5, the others offsets. `edge_count`: one partition has all 128 slots live.
All inputs are finite; a program needn't handle non-finite values. No bound on the sum of `edge_count` on one device may be relied on, other than what follows from the above.
Results may differ from a plain program's by a relative error of at most 0.02.
Values may be sent and summed in bfloat16 or wider, within the bound.
A program may use at most 128 MiB of HBM per device.

v0:
```python
import jax
import jax.numpy as jnp
from jax import lax
from jax.sharding import PartitionSpec as P


def with_halo(cells, sides, width):
    for axis, dim in sides:
        count = lax.axis_size(axis)
        head = lax.slice_in_dim(cells, 0, width, axis=dim)
        tail = lax.slice_in_dim(cells, cells.shape[dim] - width, cells.shape[dim], axis=dim)
        cells = jnp.concatenate(
            [
                lax.ppermute(tail, axis, [(i, (i + 1) % count) for i in range(count)]),
                cells,
                lax.ppermute(head, axis, [((i + 1) % count, i) for i in range(count)]),
            ],
            axis=dim,
        )
    return cells


def passed_along(value, axis, steps):
    count = lax.axis_size(axis)
    initial, last = (max(0, -steps), min(count, count - steps))
    return lax.ppermute(value, axis, [(source, source + steps) for source in range(initial, last)])


def for_sending(shard):

    def short(part):
        return part.astype(jnp.bfloat16) if part.dtype == jnp.float32 else part

    return jax.tree.map(short, shard)


def layer_norm(values):
    average = jnp.mean(values, -1, keepdims=True)
    centred = values - average
    return centred * lax.rsqrt(jnp.mean(centred * centred, -1, keepdims=True) + 1e-05)


def layer_local(node_rows, halo_rows, edge_rows, probes, weights, graph_lists):
    edge_w1, edge_w2, node_w1, node_w2, vectors = weights
    sender_row, receiver_row, live_mask = graph_lists
    coeffs = vectors.astype(jnp.float32)
    node_half = node_rows.astype(jnp.bfloat16)
    node_table = jnp.concatenate([node_half, halo_rows.astype(jnp.bfloat16)], 0)
    pick_send = (
        sender_row[:, None] == jnp.arange(node_table.shape[0], dtype=jnp.int32)[None, :]
    ).astype(jnp.bfloat16)
    pick_recv = (
        receiver_row[:, None] == jnp.arange(node_rows.shape[0], dtype=jnp.int32)[None, :]
    ).astype(jnp.bfloat16)
    senders = jnp.dot(pick_send, node_table, preferred_element_type=jnp.float32).astype(
        jnp.bfloat16
    )
    receivers = jnp.dot(pick_recv, node_half, preferred_element_type=jnp.float32).astype(
        jnp.bfloat16
    )
    joined = jnp.concatenate([edge_rows.astype(jnp.bfloat16), senders, receivers], 1)
    edge_pre = jnp.dot(joined, edge_w1, preferred_element_type=jnp.float32) + coeffs[0] + probes[0]
    edge_hid = jax.nn.silu(edge_pre).astype(jnp.bfloat16)
    edge_lin = (
        jnp.dot(edge_hid, edge_w2, preferred_element_type=jnp.float32) + coeffs[1] + probes[1]
    )
    edge_norm = layer_norm(edge_lin)
    message = (edge_norm * coeffs[2] + coeffs[3] + probes[2]) * live_mask[:, None]
    edge_next = edge_rows + message
    incoming = lax.dot_general(
        pick_recv,
        message.astype(jnp.bfloat16),
        (((0,), (0,)), ((), ())),
        preferred_element_type=jnp.float32,
    )
    node_cat = jnp.concatenate([node_half, incoming.astype(jnp.bfloat16)], 1)
    node_pre = (
        jnp.dot(node_cat, node_w1, preferred_element_type=jnp.float32) + coeffs[4] + probes[3]
    )
    node_hid = jax.nn.silu(node_pre).astype(jnp.bfloat16)
    node_lin = (
        jnp.dot(node_hid, node_w2, preferred_element_type=jnp.float32) + coeffs[5] + probes[4]
    )
    node_norm = layer_norm(node_lin)
    node_next = node_rows + node_norm * coeffs[6] + coeffs[7] + probes[5]
    return ((node_next, edge_next), (joined, edge_hid, edge_norm, node_cat, node_hid, node_norm))


def blank_probes(node_count, edge_total, features):
    edge_zero = jnp.zeros((edge_total, features), jnp.float32)
    node_zero = jnp.zeros((node_count, features), jnp.float32)
    return (edge_zero, edge_zero, edge_zero, node_zero, node_zero, node_zero)


def transposed(left, cotangent):
    return lax.dot_general(
        left,
        cotangent.astype(jnp.bfloat16),
        (((0,), (0,)), ((), ())),
        preferred_element_type=jnp.float32,
    )


def weight_grads(saved, probe_back):
    joined, edge_hid, edge_norm, node_cat, node_hid, node_norm = saved
    edge_pre_back, edge_lin_back, message_back, node_pre_back, node_lin_back, node_out_back = (
        probe_back
    )
    vector_back = jnp.stack(
        [
            edge_pre_back.sum(0),
            edge_lin_back.sum(0),
            (message_back * edge_norm).sum(0),
            message_back.sum(0),
            node_pre_back.sum(0),
            node_lin_back.sum(0),
            (node_out_back * node_norm).sum(0),
            node_out_back.sum(0),
        ],
        0,
    )
    return (
        transposed(joined, edge_pre_back),
        transposed(edge_hid, edge_lin_back),
        transposed(node_cat, node_pre_back),
        transposed(node_hid, node_lin_back),
        vector_back,
    )


def arrived(padded, margin):
    return jnp.concatenate([padded[:margin], padded[-margin:]], 0)


def keep_slot(buffer, value, keep_index, active):
    current = lax.dynamic_index_in_dim(buffer, keep_index, 0, keepdims=False)
    return lax.dynamic_update_index_in_dim(buffer, jnp.where(active, value, current), keep_index, 0)


def flatten_rows(buffer):
    return buffer.reshape(-1, buffer.shape[-1])


def local(
    node_in,
    edge_in,
    node_cot,
    edge_cot,
    send_rows,
    sender_row,
    receiver_row,
    edge_count,
    edge_w1,
    edge_w2,
    node_w1,
    node_w2,
    vectors,
):
    segment_count = lax.axis_size("segment")
    segment_index = lax.axis_index("segment")
    micro_count = node_in.shape[0]
    node_count = node_in.shape[1]
    edge_total = edge_in.shape[1]
    features = node_in.shape[2]
    margin = send_rows.shape[0] // 2
    live_mask = (jnp.arange(edge_total, dtype=jnp.int32) < edge_count[0]).astype(jnp.float32)
    weights = (edge_w1[0], edge_w2[0], node_w1[0], node_w2[0], vectors[0])
    graph_lists = (sender_row, receiver_row, live_mask)
    probes = blank_probes(node_count, edge_total, features)
    step_count = segment_count + micro_count - 1

    def local_layer(node_rows, halo_rows, edge_rows, probe_rows):
        return layer_local(node_rows, halo_rows, edge_rows, probe_rows, weights, graph_lists)

    def forward_run(operands):
        node_half, halo_half, edge_half = operands
        results, saved = layer_local(
            node_half.astype(jnp.float32),
            halo_half.astype(jnp.float32),
            edge_half.astype(jnp.float32),
            probes,
            weights,
            graph_lists,
        )
        return (results[0].astype(jnp.bfloat16), results[1].astype(jnp.bfloat16))

    def forward_skip(operands):
        return (jnp.zeros_like(operands[0]), jnp.zeros_like(operands[2]))

    node_keep = jnp.zeros_like(node_in)
    edge_keep = jnp.zeros_like(edge_in)
    halo_store = jnp.zeros((micro_count, 2 * margin, features), jnp.bfloat16)
    node_act = jnp.zeros_like(node_in)
    edge_act = jnp.zeros_like(edge_in)
    node_carry = jnp.zeros_like(node_in[0])
    edge_carry = jnp.zeros_like(edge_in[0])
    for step_number in range(step_count):
        slot_index = step_number - segment_index
        active = (slot_index >= 0) & (slot_index < micro_count)
        keep_index = jnp.clip(slot_index, 0, micro_count - 1)
        first_input = min(step_number, micro_count - 1)
        node_half = jnp.where(segment_index == 0, node_in[first_input], node_carry)
        edge_half = jnp.where(segment_index == 0, edge_in[first_input], edge_carry)
        padded = with_halo(jnp.take(node_half, send_rows, axis=0), (("dom", 0),), margin)
        halo_half = arrived(padded, margin)
        node_next, edge_next = lax.cond(
            active, forward_run, forward_skip, (node_half, halo_half, edge_half)
        )
        node_keep = keep_slot(node_keep, node_half, keep_index, active)
        edge_keep = keep_slot(edge_keep, edge_half, keep_index, active)
        halo_store = keep_slot(halo_store, halo_half, keep_index, active)
        node_act = keep_slot(node_act, node_next, keep_index, active)
        edge_act = keep_slot(edge_act, edge_next, keep_index, active)
        node_carry, edge_carry = passed_along((node_next, edge_next), "segment", 1)

    def backward_run(operands):
        node_half, halo_half, edge_half, node_out_back, edge_out_back = operands
        results, pullback, saved = jax.vjp(
            local_layer,
            node_half.astype(jnp.float32),
            halo_half.astype(jnp.float32),
            edge_half.astype(jnp.float32),
            probes,
            has_aux=True,
        )
        node_back, halo_back, edge_back, probe_back = pullback((node_out_back, edge_out_back))
        return (node_back, halo_back, edge_back, saved, probe_back)

    edge_shape = (edge_total, features)
    node_shape = (node_count, features)
    saved_zeros = (
        jnp.zeros((edge_total, 3 * features), jnp.bfloat16),
        jnp.zeros(edge_shape, jnp.bfloat16),
        jnp.zeros(edge_shape, jnp.float32),
        jnp.zeros((node_count, 2 * features), jnp.bfloat16),
        jnp.zeros(node_shape, jnp.bfloat16),
        jnp.zeros(node_shape, jnp.float32),
    )
    probe_zeros = (
        jnp.zeros(edge_shape, jnp.float32),
        jnp.zeros(edge_shape, jnp.float32),
        jnp.zeros(edge_shape, jnp.float32),
        jnp.zeros(node_shape, jnp.float32),
        jnp.zeros(node_shape, jnp.float32),
        jnp.zeros(node_shape, jnp.float32),
    )

    def backward_skip(operands):
        return (
            jnp.zeros(node_shape, jnp.float32),
            jnp.zeros((2 * margin, features), jnp.float32),
            jnp.zeros(edge_shape, jnp.float32),
            saved_zeros,
            probe_zeros,
        )

    saved_store = tuple(
        (jnp.zeros((micro_count,) + value.shape, value.dtype) for value in saved_zeros)
    )
    probe_store = tuple(
        (jnp.zeros((micro_count,) + value.shape, value.dtype) for value in probe_zeros)
    )
    node_grads = jnp.zeros((micro_count, node_count, features), jnp.float32)
    edge_grads = jnp.zeros((micro_count, edge_total, features), jnp.float32)
    node_back_carry = jnp.zeros(node_shape, jnp.float32)
    edge_back_carry = jnp.zeros(edge_shape, jnp.float32)
    is_last = segment_index == segment_count - 1
    for step_number in range(step_count):
        slot_index = step_number - (segment_count - 1 - segment_index)
        active = (slot_index >= 0) & (slot_index < micro_count)
        keep_index = jnp.clip(slot_index, 0, micro_count - 1)
        first_input = min(step_number, micro_count - 1)
        node_out_back = jnp.where(
            is_last, node_cot[first_input].astype(jnp.float32), node_back_carry
        )
        edge_out_back = jnp.where(
            is_last, edge_cot[first_input].astype(jnp.float32), edge_back_carry
        )
        node_half = lax.dynamic_index_in_dim(node_keep, keep_index, 0, keepdims=False)
        edge_half = lax.dynamic_index_in_dim(edge_keep, keep_index, 0, keepdims=False)
        halo_half = lax.dynamic_index_in_dim(halo_store, keep_index, 0, keepdims=False)
        node_back, halo_back, edge_back, saved, probe_back = lax.cond(
            active,
            backward_run,
            backward_skip,
            (node_half, halo_half, edge_half, node_out_back, edge_out_back),
        )
        returned = with_halo(for_sending(halo_back), (("dom", 0),), margin).astype(halo_back.dtype)
        node_back = node_back + jnp.zeros_like(node_back).at[send_rows].add(
            arrived(returned, margin)
        )
        saved_store = tuple(
            (
                keep_slot(buffer, value, keep_index, active)
                for buffer, value in zip(saved_store, saved)
            )
        )
        probe_store = tuple(
            (
                keep_slot(buffer, value, keep_index, active)
                for buffer, value in zip(probe_store, probe_back)
            )
        )
        node_grads = keep_slot(node_grads, node_back, keep_index, active)
        edge_grads = keep_slot(edge_grads, edge_back, keep_index, active)
        node_back_carry, edge_back_carry = passed_along((node_back, edge_back), "segment", -1)
    totals = weight_grads(
        tuple((flatten_rows(buffer) for buffer in saved_store)),
        tuple((flatten_rows(buffer) for buffer in probe_store)),
    )
    reduced = (
        lax.psum_scatter(totals[0], ("dom", "dp"), scatter_dimension=1, tiled=True),
        lax.psum_scatter(totals[1], ("dom", "dp"), scatter_dimension=1, tiled=True),
        lax.psum_scatter(totals[2], ("dom", "dp"), scatter_dimension=1, tiled=True),
        lax.psum_scatter(totals[3], ("dom", "dp"), scatter_dimension=1, tiled=True),
        lax.psum_scatter(totals[4], ("dom", "dp"), scatter_dimension=1, tiled=True),
    )
    return (
        node_act[None],
        edge_act[None],
        node_grads[None],
        edge_grads[None],
        reduced[0][None],
        reduced[1][None],
        reduced[2][None],
        reduced[3][None],
        reduced[4][None],
    )


def solution(mesh):
    in_specs = (
        P("dp", "dom", None),
        P("dp", "dom", None),
        P("dp", "dom", None),
        P("dp", "dom", None),
        P("dom"),
        P("dom"),
        P("dom"),
        P("dom"),
        P("segment", None, None),
        P("segment", None, None),
        P("segment", None, None),
        P("segment", None, None),
        P("segment", None, None),
    )
    out_specs = (
        P("segment", "dp", "dom", None),
        P("segment", "dp", "dom", None),
        P("segment", "dp", "dom", None),
        P("segment", "dp", "dom", None),
        P("segment", None, ("dom", "dp")),
        P("segment", None, ("dom", "dp")),
        P("segment", None, ("dom", "dp")),
        P("segment", None, ("dom", "dp")),
        P("segment", None, ("dom", "dp")),
    )
    return jax.shard_map(local, mesh=mesh, in_specs=in_specs, out_specs=out_specs, check_vma=False)
```

profile of v0, /device:TPU:1, one launch (start us, length us, event | category | flops | bytes accessed | tf_op | source)
XLA Modules:
  0.0 713.1 jit_solution(15438411726229533041)
XLA Ops:
  12.6 2.1 collective-permute-start
  14.7 6.7 collective-permute-start.1
  25.0 1.8 bitcast_convert_fusion
  27.6 10.9 %conditional.10 = (bf16[128,512]{1,0:T(8,128)(2,1)}, bf16[128,512]{1,0:T(8,128)(2,1)}) conditional(s32[]{:T(128)} %convert_element_type.865, () %tuple.120, (bf16[128,512]{1,0:T(8,128)(2,1)S(1)}, s32[128]{0:T(128)S(1)}, pred[]{:T(512)}, bf16[1,128,512]{2,1,0:T(8,128)(2,1)S(1)}, bf16[128,512]{1,0:T(8,128)(2,1)S(1)}, /*index=5*/s32[128]{0:T(128)}, ...), branch_computations={%region_0.2_spmd, %region_1.7_spmd} | conditional | flops 542245120 | bytes 8454701 | solution.py:206
  30.1 1.9 fusion.403
  33.1 2.4 fusion.406
  36.6 1.8 add_convert_fusion
  38.5 2.1 collective-permute-start.5
  48.9 4.8 collective-permute-start.4
  55.2 1.7 bitcast_dynamic-update-slice_fusion.73
  58.2 16.6 %conditional.11 = (bf16[128,512]{1,0:T(8,128)(2,1)}, bf16[128,512]{1,0:T(8,128)(2,1)}) conditional(s32[]{:T(128)} %convert_element_type.867, () %tuple.122, (bf16[128,512]{1,0:T(8,128)(2,1)S(1)}, s32[128]{0:T(128)S(1)}, s32[128]{0:T(128)S(1)}, bf16[128,512]{1,0:T(8,128)(2,1)S(1)}, bf16[128,512]{1,0:T(8,128)(2,1)}, ...), branch_computations={%region_6.8_spmd, %region_7.13_spmd} | conditional | flops 542179584 | bytes 7541320 | solution.py:206
  60.6 3.1 fusion.410
  66.1 1.9 convolution_convert_fusion.3
  68.0 2.9 fusion.413
  72.7 2.0 add_convert_fusion.2
  74.8 4.9 collective-permute-start.9
  90.4 4.8 collective-permute-start.8
  96.7 1.7 bitcast_dynamic-update-slice_fusion.72
  101.3 18.5 %collective-permute-start.13 = (bf16[128,512]{1,0:T(8,128)(2,1)}, bf16[128,512]{1,0:T(8,128)(2,1)}, u32[]{:S(2)}, u32[]{:S(2)}) collective-permute-start(bf16[128,512]{1,0:T(8,128)(2,1)} %get-tuple-element.990), channel_id=1, source_target_pairs={{0,64},{64,128},{128,192},{1,65},{65,129},{129,193},{2,66},{66,130... | collective-permute-start | bytes 393224 | tf_op jit(solution)/shard_map/ppermute | solution.py:26
  121.4 2.2 collective-permute-start.10
  130.5 4.8 collective-permute-start.12
  136.8 1.7 bitcast_dynamic-update-slice_fusion.71
  141.2 4.8 collective-permute-start.17
  146.7 16.0 %collective-permute-start.14 = (bf16[128,512]{1,0:T(8,128)(2,1)}, bf16[128,512]{1,0:T(8,128)(2,1)S(1)}, u32[]{:S(2)}, u32[]{:S(2)}) collective-permute-start(bf16[128,512]{1,0:T(8,128)(2,1)} %get-tuple-element.991), channel_id=1, source_target_pairs={{0,64},{64,128},{128,192},{1,65},{65,129},{129,193},{2,66},{66,130... | collective-permute-start | bytes 393224 | tf_op jit(solution)/shard_map/ppermute | solution.py:26
  163.4 1.7 copy.75
  167.6 1.8 gather_fusion.4
  170.5 4.8 collective-permute-start.16
  175.3 1.8 bitcast_dynamic-update-slice_fusion.70
  177.8 3.2 conditional.15
  181.0 1.7 collective-permute-start.21
  183.6 4.8 collective-permute-start.19
  207.6 3.4 scatter_custom_fusion
  213.4 5.7 collective-permute-done.20
  219.2 2.5 conditional.16
  223.2 1.7 bitcast_dynamic-update-slice_fusion.53
  225.0 4.9 collective-permute-start.23
  246.0 3.4 scatter_custom_fusion.1
  250.6 1.7 bitcast_dynamic-update-slice_fusion.58
  254.0 3.3 collective-permute-done.24
  257.3 2.5 conditional.17
  261.3 1.7 bitcast_dynamic-update-slice_fusion.52
  263.1 4.8 collective-permute-start.27
  284.0 3.4 scatter_custom_fusion.2
  288.7 1.7 bitcast_dynamic-update-slice_fusion.57
  290.4 1.7 constant_dynamic-slice_fusion.48
  292.1 28.7 %collective-permute-done.29 = f32[128,512]{1,0:T(8,128)} collective-permute-done((f32[128,512]{1,0:T(8,128)}, f32[128,512]{1,0:T(8,128)}, u32[]{:S(2)}, u32[]{:S(2)}) %collective-permute-start.29) | collective-permute-done | bytes 262176 | tf_op jit(solution)/shard_map/ppermute | solution.py:26
  320.8 30.0 %collective-permute-done.28 = f32[128,512]{1,0:T(8,128)S(1)} collective-permute-done((f32[128,512]{1,0:T(8,128)}, f32[128,512]{1,0:T(8,128)S(1)}, u32[]{:S(2)}, u32[]{:S(2)}) %collective-permute-start.28) | collective-permute-done | bytes 262176 | tf_op jit(solution)/shard_map/ppermute | solution.py:26
  350.8 16.2 %conditional.18 = (f32[128,512]{1,0:T(8,128)S(1)}, f32[128,512]{1,0:T(8,128)S(1)}, f32[128,512]{1,0:T(8,128)}, bf16[128,1536]{1,0:T(8,128)(2,1)S(1)}, bf16[128,5...) conditional(s32[]{:T(128)} %convert_element_type.884, ...), branch_computations={%region_63.65_spmd, %region_64.74_spmd} | conditional | flops 1082066432 | bytes 46409420 | solution.py:282
  357.4 1.7 multiply_reduce_fusion.24
  368.5 1.8 bitcast_dynamic-update-slice_fusion.51
  370.4 4.8 collective-permute-start.31
  377.8 1.8 constant_dynamic-slice_fusion.28
  384.7 3.4 scatter_custom_fusion.3
  391.1 1.9 copy.245
  393.0 1.8 bitcast_dynamic-update-slice_fusion.21
  396.3 13.6 %conditional.19 = (f32[128,512]{1,0:T(8,128)S(1)}, f32[128,512]{1,0:T(8,128)S(1)}, f32[128,512]{1,0:T(8,128)S(1)}, bf16[128,1536]{1,0:T(8,128)(2,1)S(1)}, bf16[1...) conditional(s32[]{:T(128)} %convert_element_type.887, ...), branch_computations={%region_74.76_spmd, %region_75.85_spmd} | conditional | flops 1082066432 | bytes 40117852 | solution.py:282
  400.6 1.7 multiply_reduce_fusion.28
  410.0 2.1 bitcast_dynamic-update-slice_fusion.25
  413.7 1.7 bitcast_dynamic-update-slice_fusion.30
  419.7 1.9 convolution_bitcast_fusion.1
  421.6 2.3 convolution_bitcast_fusion
  434.0 4.8 collective-permute-start.35
  442.5 252.8 %all-reduce.4 = f32[8,512]{1,0:T(8,128)S(1)} all-reduce(f32[8,512]{1,0:T(8,128)S(1)} %stack.35), channel_id=6, replica_groups=mesh['segment'=4,'dom'=32,'dp'=2] {'dom','dp'}, use_global_device_ids=true, to_apply=%region_97.99.clone | all-reduce | flops 4096 | bytes 32768
  695.3 1.7 bitcast_dynamic-update-slice_fusion.50
  (908 shorter events, 203.7 us)
Async XLA Ops:
  7.2 15.0 %copy-start.310 = (u32[256]{0:T(256)S(1)}, u32[256]{0:T(256)}, u32[]{:S(2)}) copy-start(u32[256]{0:T(256)} %constant.788) | copy-start | bytes 3076
  7.2 16.2 %copy-start.147 = (bf16[2,128,512]{2,1,0:T(8,128)(2,1)S(1)}, bf16[2,128,512]{2,1,0:T(8,128)(2,1)}, u32[]{:S(2)}) copy-start(bf16[2,128,512]{2,1,0:T(8,128)(2,1)} %param.36) | copy-start | bytes 786436
  7.2 693.1 %all-reduce.8.cloned.1.call-start = ((), (), s32[]{:S(2)}) async-start(), calls=%async_computation | async-start | bytes 14680064
  8.6 14.1 %copy-start.297 = (pred[128]{0:T(512)(128)(4,1)}, pred[128]{0:T(512)(128)(4,1)S(1)}, u32[]{:S(2)}) copy-start(pred[128]{0:T(512)(128)(4,1)S(1)} %compare_and_fusion) | copy-start | bytes 388
  11.8 15.7 %copy-start = (bf16[1,1536,512]{2,1,0:T(8,128)(2,1)S(1)}, bf16[1,1536,512]{2,1,0:T(8,128)(2,1)}, u32[]{:S(2)}) copy-start(bf16[1,1536,512]{2,1,0:T(8,128)(2,1)} %param.43) | copy-start | bytes 4718596
  11.8 15.7 %copy-start.1 = (bf16[1,1024,512]{2,1,0:T(8,128)(2,1)S(1)}, bf16[1,1024,512]{2,1,0:T(8,128)(2,1)}, u32[]{:S(2)}) copy-start(bf16[1,1024,512]{2,1,0:T(8,128)(2,1)} %param.45) | copy-start | bytes 3145732
  11.8 15.7 %copy-start.113 = (bf16[1,8,512]{2,1,0:T(8,128)(2,1)S(1)}, bf16[1,8,512]{2,1,0:T(8,128)(2,1)}, u32[]{:S(2)}) copy-start(bf16[1,8,512]{2,1,0:T(8,128)(2,1)} %param.47) | copy-start | bytes 24580
  11.9 15.7 %copy-start.270 = (s32[128]{0:T(128)S(1)}, s32[128]{0:T(128)}, u32[]{:S(2)}) copy-start(s32[128]{0:T(128)} %param.41) | copy-start | bytes 1540
  12.6 14.2 %collective-permute-start = (bf16[64,512]{1,0:T(8,128)(2,1)}, bf16[64,512]{1,0:T(8,128)(2,1)S(1)}, u32[]{:S(2)}, u32[]{:S(2)}) collective-permute-start(bf16[64,512]{1,0:T(8,128)(2,1)} %get-tuple-element.1345), channel_id=1, source_target_pairs={{0,2},{2,4},{4,6},{6,8},{8,10},{10,12},{12,14},{14,16},{16,18},{18... | collective-permute-start | bytes 196616 | tf_op jit(solution)/shard_map/ppermute | solution.py:14
  14.7 12.1 %collective-permute-start.1 = (bf16[64,512]{1,0:T(8,128)(2,1)}, bf16[64,512]{1,0:T(8,128)(2,1)S(1)}, u32[]{:S(2)}, u32[]{:S(2)}) collective-permute-start(bf16[64,512]{1,0:T(8,128)(2,1)} %get-tuple-element.1346), channel_id=1, source_target_pairs={{2,0},{4,2},{6,4},{8,6},{10,8},{12,10},{14,12},{16,14},{18,16},{20... | collective-permute-start | bytes 196616 | tf_op jit(solution)/shard_map/ppermute | solution.py:16
  38.5 16.7 %collective-permute-start.5 = (bf16[128,512]{1,0:T(8,128)(2,1)}, bf16[128,512]{1,0:T(8,128)(2,1)}, u32[]{:S(2)}, u32[]{:S(2)}) collective-permute-start(bf16[128,512]{1,0:T(8,128)(2,1)} %get-tuple-element.986), channel_id=1, source_target_pairs={{0,64},{64,128},{128,192},{1,65},{65,129},{129,193},{2,66},{66,130... | collective-permute-start | bytes 393224 | tf_op jit(solution)/shard_map/ppermute | solution.py:26
  41.6 3.8 collective-permute-start.2
  48.8 8.8 %collective-permute-start.3 = (bf16[64,512]{1,0:T(8,128)(2,1)S(1)}, bf16[64,512]{1,0:T(8,128)(2,1)S(1)}, u32[]{:S(2)}, u32[]{:S(2)}) collective-permute-start(bf16[64,512]{1,0:T(8,128)(2,1)S(1)} %get-tuple-element.1343), channel_id=1, source_target_pairs={{0,2},{2,4},{4,6},{6,8},{8,10},{10,12},{12,14},{14,16},{16,18},{18... | collective-permute-start | bytes 196616 | tf_op jit(solution)/shard_map/ppermute | solution.py:14
  48.9 8.7 %collective-permute-start.4 = (bf16[64,512]{1,0:T(8,128)(2,1)S(1)}, bf16[64,512]{1,0:T(8,128)(2,1)S(1)}, u32[]{:S(2)}, u32[]{:S(2)}) collective-permute-start(bf16[64,512]{1,0:T(8,128)(2,1)S(1)} %get-tuple-element.1344), channel_id=1, source_target_pairs={{2,0},{4,2},{6,4},{8,6},{10,8},{12,10},{14,12},{16,14},{18,16},{20... | collective-permute-start | bytes 196616 | tf_op jit(solution)/shard_map/ppermute | solution.py:16
  74.8 12.2 %copy-start.144 = (bf16[2,128,512]{2,1,0:T(8,128)(2,1)S(1)}, bf16[2,128,512]{2,1,0:T(8,128)(2,1)}, u32[]{:S(2)}) copy-start(bf16[2,128,512]{2,1,0:T(8,128)(2,1)} %param.35) | copy-start | bytes 786436
  74.8 12.2 %copy-start.265 = (bf16[1,128,512]{2,1,0:T(8,128)(2,1)S(1)}, bf16[1,128,512]{2,1,0:T(8,128)(2,1)}, u32[]{:S(2)}) copy-start(bf16[1,128,512]{2,1,0:T(8,128)(2,1)} %constant_dynamic-slice_fusion.59) | copy-start | bytes 393220
  74.8 22.0 %collective-permute-start.9 = (bf16[128,512]{1,0:T(8,128)(2,1)}, bf16[128,512]{1,0:T(8,128)(2,1)}, u32[]{:S(2)}, u32[]{:S(2)}) collective-permute-start(bf16[128,512]{1,0:T(8,128)(2,1)} %get-tuple-element.988), channel_id=1, source_target_pairs={{0,64},{64,128},{128,192},{1,65},{65,129},{129,193},{2,66},{66,130... | collective-permute-start | bytes 393224 | tf_op jit(solution)/shard_map/ppermute | solution.py:26
  82.1 4.8 collective-permute-start.6
  90.3 8.8 %collective-permute-start.7 = (bf16[64,512]{1,0:T(8,128)(2,1)S(1)}, bf16[64,512]{1,0:T(8,128)(2,1)S(1)}, u32[]{:S(2)}, u32[]{:S(2)}) collective-permute-start(bf16[64,512]{1,0:T(8,128)(2,1)S(1)} %get-tuple-element.1341), channel_id=1, source_target_pairs={{0,2},{2,4},{4,6},{6,8},{8,10},{10,12},{12,14},{14,16},{16,18},{18... | collective-permute-start | bytes 196616 | tf_op jit(solution)/shard_map/ppermute | solution.py:14
  90.4 8.7 %collective-permute-start.8 = (bf16[64,512]{1,0:T(8,128)(2,1)S(1)}, bf16[64,512]{1,0:T(8,128)(2,1)S(1)}, u32[]{:S(2)}, u32[]{:S(2)}) collective-permute-start(bf16[64,512]{1,0:T(8,128)(2,1)S(1)} %get-tuple-element.1342), channel_id=1, source_target_pairs={{2,0},{4,2},{6,4},{8,6},{10,8},{12,10},{14,12},{16,14},{18,16},{20... | collective-permute-start | bytes 196616 | tf_op jit(solution)/shard_map/ppermute | solution.py:16
  101.2 25.8 %copy-start.145 = (bf16[2,128,512]{2,1,0:T(8,128)(2,1)S(1)}, bf16[2,128,512]{2,1,0:T(8,128)(2,1)}, u32[]{:S(2)}) copy-start(bf16[2,128,512]{2,1,0:T(8,128)(2,1)} %param.35) | copy-start | bytes 786436
  101.2 25.8 %copy-start.267 = (bf16[1,128,512]{2,1,0:T(8,128)(2,1)S(1)}, bf16[1,128,512]{2,1,0:T(8,128)(2,1)}, u32[]{:S(2)}) copy-start(bf16[1,128,512]{2,1,0:T(8,128)(2,1)} %constant_dynamic-slice_fusion.58) | copy-start | bytes 393220
  101.3 35.6 %collective-permute-start.13 = (bf16[128,512]{1,0:T(8,128)(2,1)}, bf16[128,512]{1,0:T(8,128)(2,1)}, u32[]{:S(2)}, u32[]{:S(2)}) collective-permute-start(bf16[128,512]{1,0:T(8,128)(2,1)} %get-tuple-element.990), channel_id=1, source_target_pairs={{0,64},{64,128},{128,192},{1,65},{65,129},{129,193},{2,66},{66,130... | collective-permute-start | bytes 393224 | tf_op jit(solution)/shard_map/ppermute | solution.py:26
  121.4 5.6 collective-permute-start.10
  130.4 8.8 %collective-permute-start.11 = (bf16[64,512]{1,0:T(8,128)(2,1)S(1)}, bf16[64,512]{1,0:T(8,128)(2,1)S(1)}, u32[]{:S(2)}, u32[]{:S(2)}) collective-permute-start(bf16[64,512]{1,0:T(8,128)(2,1)S(1)} %get-tuple-element.1339), channel_id=1, source_target_pairs={{0,2},{2,4},{4,6},{6,8},{8,10},{10,12},{12,14},{14,16},{16,18},{18... | collective-permute-start | bytes 196616 | tf_op jit(solution)/shard_map/ppermute | solution.py:14
  130.5 8.7 %collective-permute-start.12 = (bf16[64,512]{1,0:T(8,128)(2,1)S(1)}, bf16[64,512]{1,0:T(8,128)(2,1)S(1)}, u32[]{:S(2)}, u32[]{:S(2)}) collective-permute-start(bf16[64,512]{1,0:T(8,128)(2,1)S(1)} %get-tuple-element.1340), channel_id=1, source_target_pairs={{2,0},{4,2},{6,4},{8,6},{10,8},{12,10},{14,12},{16,14},{18,16},{20... | collective-permute-start | bytes 196616 | tf_op jit(solution)/shard_map/ppermute | solution.py:16
  141.2 25.6 %copy-start.283 = (bf16[64,512]{1,0:T(8,128)(2,1)S(1)}, bf16[64,512]{1,0:T(8,128)(2,1)}, u32[]{:S(2)}) copy-start(bf16[64,512]{1,0:T(8,128)(2,1)} %copy-done.282) | copy-start | bytes 196612
  141.2 25.6 %copy-start.287 = (bf16[64,512]{1,0:T(8,128)(2,1)S(1)}, bf16[64,512]{1,0:T(8,128)(2,1)}, u32[]{:S(2)}) copy-start(bf16[64,512]{1,0:T(8,128)(2,1)} %copy-done.286) | copy-start | bytes 196612
  141.2 25.6 %copy-start.146 = (bf16[2,128,512]{2,1,0:T(8,128)(2,1)S(1)}, bf16[2,128,512]{2,1,0:T(8,128)(2,1)}, u32[]{:S(2)}) copy-start(bf16[2,128,512]{2,1,0:T(8,128)(2,1)} %param.35) | copy-start | bytes 786436
  141.2 25.6 %copy-start.268 = (bf16[1,128,512]{2,1,0:T(8,128)(2,1)S(1)}, bf16[1,128,512]{2,1,0:T(8,128)(2,1)}, u32[]{:S(2)}) copy-start(bf16[1,128,512]{2,1,0:T(8,128)(2,1)} %constant_dynamic-slice_fusion.57) | copy-start | bytes 393220
  141.2 34.1 %collective-permute-start.17 = (bf16[128,512]{1,0:T(8,128)(2,1)}, bf16[128,512]{1,0:T(8,128)(2,1)}, u32[]{:S(2)}, u32[]{:S(2)}) collective-permute-start(bf16[128,512]{1,0:T(8,128)(2,1)} %get-tuple-element.992), channel_id=1, source_target_pairs={{0,64},{64,128},{128,192},{1,65},{65,129},{129,193},{2,66},{66,130... | collective-permute-start | bytes 393224 | tf_op jit(solution)/shard_map/ppermute | solution.py:26
  146.7 20.1 %collective-permute-start.14 = (bf16[128,512]{1,0:T(8,128)(2,1)}, bf16[128,512]{1,0:T(8,128)(2,1)S(1)}, u32[]{:S(2)}, u32[]{:S(2)}) collective-permute-start(bf16[128,512]{1,0:T(8,128)(2,1)} %get-tuple-element.991), channel_id=1, source_target_pairs={{0,64},{64,128},{128,192},{1,65},{65,129},{129,193},{2,66},{66,130... | collective-permute-start | bytes 393224 | tf_op jit(solution)/shard_map/ppermute | solution.py:26
  170.4 6.6 collective-permute-start.15
  170.5 6.5 collective-permute-start.16
  181.0 32.4 %collective-permute-start.21 = (f32[128,512]{1,0:T(8,128)}, f32[128,512]{1,0:T(8,128)}, u32[]{:S(2)}, u32[]{:S(2)}) collective-permute-start(f32[128,512]{1,0:T(8,128)} %get-tuple-element.997), channel_id=1, source_target_pairs={{64,0},{128,64},{192,128},{65,1},{129,65},{193,129},{66,2},{130,66... | collective-permute-start | bytes 786440 | tf_op jit(solution)/shard_map/ppermute | solution.py:26
  182.8 15.2 %copy-start.82 = (f32[2,128,512]{2,1,0:T(8,128)}, f32[2,128,512]{2,1,0:T(8,128)S(1)}, u32[]{:S(2)}) copy-start(f32[2,128,512]{2,1,0:T(8,128)S(1)} %bitcast_dynamic-update-slice_fusion.54) | copy-start | bytes 1572868
  183.6 22.4 %collective-permute-start.18 = (bf16[64,512]{1,0:T(8,128)(2,1)}, bf16[64,512]{1,0:T(8,128)(2,1)}, u32[]{:S(2)}, u32[]{:S(2)}) collective-permute-start(bf16[64,512]{1,0:T(8,128)(2,1)} %get-tuple-element.1335), channel_id=1, source_target_pairs={{0,2},{2,4},{4,6},{6,8},{8,10},{10,12},{12,14},{14,16},{16,18},{18... | collective-permute-start | bytes 196616 | tf_op jit(solution)/shard_map/ppermute | solution.py:14
  183.6 22.4 %collective-permute-start.19 = (bf16[64,512]{1,0:T(8,128)(2,1)}, bf16[64,512]{1,0:T(8,128)(2,1)}, u32[]{:S(2)}, u32[]{:S(2)}) collective-permute-start(bf16[64,512]{1,0:T(8,128)(2,1)} %get-tuple-element.1336), channel_id=1, source_target_pairs={{2,0},{4,2},{6,4},{8,6},{10,8},{12,10},{14,12},{16,14},{18,16},{20... | collective-permute-start | bytes 196616 | tf_op jit(solution)/shard_map/ppermute | solution.py:16
  204.5 14.6 %copy-start.110 = (pred[128,512]{1,0:T(32,128)(4,1)S(1)}, pred[128,512]{1,0:T(32,128)(4,1)}, u32[]{:S(2)}) copy-start(pred[128,512]{1,0:T(32,128)(4,1)} %copy-done.109) | copy-start | bytes 196612
  204.5 14.6 %copy-start.292 = (s32[128]{0:T(128)S(1)}, s32[128]{0:T(128)}, u32[]{:S(2)}) copy-start(s32[128]{0:T(128)} %param.40) | copy-start | bytes 1540
  211.0 8.1 %collective-permute-start.20 = (f32[128,512]{1,0:T(8,128)}, f32[128,512]{1,0:T(8,128)S(1)}, u32[]{:S(2)}, u32[]{:S(2)}) collective-permute-start(f32[128,512]{1,0:T(8,128)} %scatter_custom_fusion), channel_id=1, source_target_pairs={{64,0},{128,64},{192,128},{65,1},{129,65},{193,129},{66,2},{130,66... | collective-permute-start | bytes 786440 | tf_op jit(solution)/shard_map/ppermute | solution.py:26
  221.7 12.3 %copy-start.223 = (f32[128,512]{1,0:T(8,128)}, f32[128,512]{1,0:T(8,128)S(1)}, u32[]{:S(2)}) copy-start(f32[128,512]{1,0:T(8,128)S(1)} %get-tuple-element.998) | copy-start | bytes 786436
  221.7 12.2 %copy-start.3 = (f32[2,128,512]{2,1,0:T(8,128)S(1)}, f32[2,128,512]{2,1,0:T(8,128)}, u32[]{:S(2)}) copy-start(f32[2,128,512]{2,1,0:T(8,128)} %copy-done.2) | copy-start | bytes 1572868
  221.7 12.2 %copy-start.186 = (f32[1,128,512]{2,1,0:T(8,128)S(1)}, f32[1,128,512]{2,1,0:T(8,128)}, u32[]{:S(2)}) copy-start(f32[1,128,512]{2,1,0:T(8,128)} %constant_dynamic-slice_fusion.31) | copy-start | bytes 786436
  221.7 32.3 %collective-permute-start.25 = (f32[128,512]{1,0:T(8,128)}, f32[128,512]{1,0:T(8,128)}, u32[]{:S(2)}, u32[]{:S(2)}) collective-permute-start(f32[128,512]{1,0:T(8,128)} %get-tuple-element.1000), channel_id=1, source_target_pairs={{64,0},{128,64},{192,128},{65,1},{129,65},{193,129},{66,2},{130,66... | collective-permute-start | bytes 786440 | tf_op jit(solution)/shard_map/ppermute | solution.py:26
  224.9 20.3 %collective-permute-start.22 = (bf16[64,512]{1,0:T(8,128)(2,1)S(1)}, bf16[64,512]{1,0:T(8,128)(2,1)S(1)}, u32[]{:S(2)}, u32[]{:S(2)}) collective-permute-start(bf16[64,512]{1,0:T(8,128)(2,1)S(1)} %get-tuple-element.1333), channel_id=1, source_target_pairs={{0,2},{2,4},{4,6},{6,8},{8,10},{10,12},{12,14},{14,16},{16,18},{18... | collective-permute-start | bytes 196616 | tf_op jit(solution)/shard_map/ppermute | solution.py:14
  225.0 20.2 %collective-permute-start.23 = (bf16[64,512]{1,0:T(8,128)(2,1)S(1)}, bf16[64,512]{1,0:T(8,128)(2,1)S(1)}, u32[]{:S(2)}, u32[]{:S(2)}) collective-permute-start(bf16[64,512]{1,0:T(8,128)(2,1)S(1)} %get-tuple-element.1334), channel_id=1, source_target_pairs={{2,0},{4,2},{6,4},{8,6},{10,8},{12,10},{14,12},{16,14},{18,16},{20... | collective-permute-start | bytes 196616 | tf_op jit(solution)/shard_map/ppermute | solution.py:16
  249.3 7.9 %collective-permute-start.24 = (f32[128,512]{1,0:T(8,128)}, f32[128,512]{1,0:T(8,128)S(1)}, u32[]{:S(2)}, u32[]{:S(2)}) collective-permute-start(f32[128,512]{1,0:T(8,128)} %scatter_custom_fusion.1), channel_id=1, source_target_pairs={{64,0},{128,64},{192,128},{65,1},{129,65},{193,129},{66,2},{130,66... | collective-permute-start | bytes 786440 | tf_op jit(solution)/shard_map/ppermute | solution.py:26
  259.8 12.1 %copy-start.228 = (f32[128,512]{1,0:T(8,128)}, f32[128,512]{1,0:T(8,128)S(1)}, u32[]{:S(2)}) copy-start(f32[128,512]{1,0:T(8,128)S(1)} %get-tuple-element.1001) | copy-start | bytes 786436
  259.9 12.1 %copy-start.5 = (f32[2,128,512]{2,1,0:T(8,128)S(1)}, f32[2,128,512]{2,1,0:T(8,128)}, u32[]{:S(2)}) copy-start(f32[2,128,512]{2,1,0:T(8,128)} %copy-done.4) | copy-start | bytes 1572868
  259.9 60.9 %collective-permute-start.29 = (f32[128,512]{1,0:T(8,128)}, f32[128,512]{1,0:T(8,128)}, u32[]{:S(2)}, u32[]{:S(2)}) collective-permute-start(f32[128,512]{1,0:T(8,128)} %get-tuple-element.1003), channel_id=1, source_target_pairs={{64,0},{128,64},{192,128},{65,1},{129,65},{193,129},{66,2},{130,66... | collective-permute-start | bytes 786440 | tf_op jit(solution)/shard_map/ppermute | solution.py:26
  263.1 20.2 %collective-permute-start.26 = (bf16[64,512]{1,0:T(8,128)(2,1)S(1)}, bf16[64,512]{1,0:T(8,128)(2,1)S(1)}, u32[]{:S(2)}, u32[]{:S(2)}) collective-permute-start(bf16[64,512]{1,0:T(8,128)(2,1)S(1)} %get-tuple-element.1331), channel_id=1, source_target_pairs={{0,2},{2,4},{4,6},{6,8},{8,10},{10,12},{12,14},{14,16},{16,18},{18... | collective-permute-start | bytes 196616 | tf_op jit(solution)/shard_map/ppermute | solution.py:14
  263.1 20.1 %collective-permute-start.27 = (bf16[64,512]{1,0:T(8,128)(2,1)S(1)}, bf16[64,512]{1,0:T(8,128)(2,1)S(1)}, u32[]{:S(2)}, u32[]{:S(2)}) collective-permute-start(bf16[64,512]{1,0:T(8,128)(2,1)S(1)} %get-tuple-element.1332), channel_id=1, source_target_pairs={{2,0},{4,2},{6,4},{8,6},{10,8},{12,10},{14,12},{16,14},{18,16},{20... | collective-permute-start | bytes 196616 | tf_op jit(solution)/shard_map/ppermute | solution.py:16
  287.4 63.4 %collective-permute-start.28 = (f32[128,512]{1,0:T(8,128)}, f32[128,512]{1,0:T(8,128)S(1)}, u32[]{:S(2)}, u32[]{:S(2)}) collective-permute-start(f32[128,512]{1,0:T(8,128)} %scatter_custom_fusion.2), channel_id=1, source_target_pairs={{64,0},{128,64},{192,128},{65,1},{129,65},{193,129},{66,2},{130,66... | collective-permute-start | bytes 786440 | tf_op jit(solution)/shard_map/ppermute | solution.py:26
  367.1 27.7 %collective-permute-start.33 = (f32[128,512]{1,0:T(8,128)}, f32[128,512]{1,0:T(8,128)}, u32[]{:S(2)}, u32[]{:S(2)}) collective-permute-start(f32[128,512]{1,0:T(8,128)} %get-tuple-element.1006), channel_id=1, source_target_pairs={{64,0},{128,64},{192,128},{65,1},{129,65},{193,129},{66,2},{130,66... | collective-permute-start | bytes 786440 | tf_op jit(solution)/shard_map/ppermute | solution.py:26
  370.3 13.6 %collective-permute-start.30 = (bf16[64,512]{1,0:T(8,128)(2,1)S(1)}, bf16[64,512]{1,0:T(8,128)(2,1)S(1)}, u32[]{:S(2)}, u32[]{:S(2)}) collective-permute-start(bf16[64,512]{1,0:T(8,128)(2,1)S(1)} %get-tuple-element.1329), channel_id=1, source_target_pairs={{0,2},{2,4},{4,6},{6,8},{8,10},{10,12},{12,14},{14,16},{16,18},{18... | collective-permute-start | bytes 196616 | tf_op jit(solution)/shard_map/ppermute | solution.py:14
  370.4 13.5 %collective-permute-start.31 = (bf16[64,512]{1,0:T(8,128)(2,1)S(1)}, bf16[64,512]{1,0:T(8,128)(2,1)S(1)}, u32[]{:S(2)}, u32[]{:S(2)}) collective-permute-start(bf16[64,512]{1,0:T(8,128)(2,1)S(1)} %get-tuple-element.1330), channel_id=1, source_target_pairs={{2,0},{4,2},{6,4},{8,6},{10,8},{12,10},{14,12},{16,14},{18,16},{20... | collective-permute-start | bytes 196616 | tf_op jit(solution)/shard_map/ppermute | solution.py:16
  388.1 8.2 %collective-permute-start.32 = (f32[128,512]{1,0:T(8,128)}, f32[128,512]{1,0:T(8,128)S(1)}, u32[]{:S(2)}, u32[]{:S(2)}) collective-permute-start(f32[128,512]{1,0:T(8,128)} %scatter_custom_fusion.3), channel_id=1, source_target_pairs={{64,0},{128,64},{192,128},{65,1},{129,65},{193,129},{66,2},{130,66... | collective-permute-start | bytes 786440 | tf_op jit(solution)/shard_map/ppermute | solution.py:26
  433.9 263.8 %collective-permute-start.34 = (bf16[64,512]{1,0:T(8,128)(2,1)S(1)}, bf16[64,512]{1,0:T(8,128)(2,1)}, u32[]{:S(2)}, u32[]{:S(2)}) collective-permute-start(bf16[64,512]{1,0:T(8,128)(2,1)S(1)} %get-tuple-element.1327), channel_id=1, source_target_pairs={{0,2},{2,4},{4,6},{6,8},{8,10},{10,12},{12,14},{14,16},{16,18},{18... | collective-permute-start | bytes 196616 | tf_op jit(solution)/shard_map/ppermute | solution.py:14
  434.0 263.7 %collective-permute-start.35 = (bf16[64,512]{1,0:T(8,128)(2,1)S(1)}, bf16[64,512]{1,0:T(8,128)(2,1)}, u32[]{:S(2)}, u32[]{:S(2)}) collective-permute-start(bf16[64,512]{1,0:T(8,128)(2,1)S(1)} %get-tuple-element.1328), channel_id=1, source_target_pairs={{2,0},{4,2},{6,4},{8,6},{10,8},{12,10},{14,12},{16,14},{18,16},{20... | collective-permute-start | bytes 196616 | tf_op jit(solution)/shard_map/ppermute | solution.py:16
  441.7 253.6 %copy-start.85 = (f32[2,128,512]{2,1,0:T(8,128)S(1)}, f32[2,128,512]{2,1,0:T(8,128)}, u32[]{:S(2)}) copy-start(f32[2,128,512]{2,1,0:T(8,128)} %bitcast_dynamic-update-slice_fusion.51) | copy-start | bytes 1572868
  441.8 256.8 %copy-start.245 = (f32[128,512]{1,0:T(8,128)S(1)}, f32[128,512]{1,0:T(8,128)}, u32[]{:S(2)}) copy-start(f32[128,512]{1,0:T(8,128)} %copy-done.244) | copy-start | bytes 786436
  441.8 258.4 %copy-start.73 = (f32[2,128,512]{2,1,0:T(8,128)S(1)}, f32[2,128,512]{2,1,0:T(8,128)}, u32[]{:S(2)}) copy-start(f32[2,128,512]{2,1,0:T(8,128)} %copy-done.72) | copy-start | bytes 1572868
  442.0 258.2 %copy-start.263 = (f32[1,2,128,512]{3,2,1,0:T(8,128)S(1)}, f32[1,2,128,512]{3,2,1,0:T(8,128)}, u32[]{:S(2)}) copy-start(f32[1,2,128,512]{3,2,1,0:T(8,128)} %copy.240) | copy-start | bytes 1572868
  (217 other events, 718.6 us)
Sparse Core Ops, SparseCore 0:
  424.0 207.7 all-reduce.7
where the time goes:
time: 726 us; the launch traced here: 713 us
  blocking collectives  253 us (35%)
  starting transfers between devices  115 us (16%)
  local copies, waits for them, and re-layouts  112 us (15%)
  other arithmetic  102 us (14%)
  waiting for transfers between devices  71.6 us (10%)
  matrix products  39.9 us (5%)
  between operations  18.5 us (3%)
    unnamed x1, blocking collectives  253 us
    ppermute x16, waiting for transfers between devices, passed_along(): lax.ppermute(value, axis, [(source, source + steps) for source in range(i...  71.5 us
    ppermute x16, starting transfers between devices, passed_along(): lax.ppermute(value, axis, [(source, source + steps) for source in range(i...  62.5 us
    dynamic_slice x67, local copies, waits for them, and re-layouts, keep_slot(): current = lax.dynamic_index_in_dim(buffer, keep_index, 0, keepdims=False)  57 us
    dynamic_update_slice x95, other arithmetic, keep_slot(): lax.dynamic_update_index_in_dim(buffer, jnp.where(active, value, current)...  54.6 us
    ppermute x10, starting transfers between devices, with_halo(): lax.ppermute(head, axis, [((i + 1) % count, i) for i in range(count)])  49.8 us
    unnamed x411, local copies, waits for them, and re-layouts  20.7 us
    scatter-add x5, other arithmetic, local(): jnp.zeros_like(node_back).at[send_rows].add(arrived(returned, margin))  15.2 us
  transfers between devices with their start and end apart: 37, of which 7 were waited for; matrix products, arithmetic and copies ran while one was open for 21% of the time, Pallas kernels for 0%

commit v1 on v0

v1 whole, which is shorter than its diff:
```python
import functools

import jax
import jax.numpy as jnp
from jax import lax
from jax.experimental import pallas as pl
from jax.experimental.pallas import tpu as pltpu
from jax.sharding import PartitionSpec as P

F32 = jnp.float32
BF16 = jnp.bfloat16
MESH = pl.DeviceIdType.MESH

D = 512
ROWS = 128
HALO = 64
SAMPLES = 2
NY = 4
NZ = 8
DOMS = NY * NZ
SECTIONS = 4
HALF = 1920
LANES_A = 1280
LANES_B = HALF - LANES_A


def dot_nn(left, right):
    return jnp.dot(left, right, preferred_element_type=F32)


def dot_nt(left, right):
    return lax.dot_general(left, right, (((1,), (1,)), ((), ())), preferred_element_type=F32)


def sigmoid(values):
    return 0.5 * jnp.tanh(0.5 * values) + 0.5


def norm_parts(values):
    average = jnp.mean(values, -1, keepdims=True)
    centred = values - average
    scale = lax.rsqrt(jnp.mean(centred * centred, -1, keepdims=True) + 1e-05)
    return centred * scale, scale


def norm_back(cotangent, normed, scale):
    first = jnp.mean(cotangent, -1, keepdims=True)
    second = jnp.mean(cotangent * normed, -1, keepdims=True)
    return scale * (cotangent - first - normed * second)


def column_sum(values):
    return jnp.sum(values, 0, keepdims=True)


def kernel(
    node_in,
    edge_in,
    node_cot,
    edge_cot,
    send_rows,
    sender_row,
    receiver_row,
    edge_count,
    w1e_hbm,
    w2e_hbm,
    w1n_hbm,
    w2n_hbm,
    vectors,
    node_out,
    edge_out,
    node_grad,
    edge_grad,
    grads_out,
    w1e,
    w2e,
    w1n,
    w2n,
    coeffs,
    table,
    edge_x,
    node_x,
    snd,
    rcv,
    hid_e,
    pre_e,
    norm_e,
    scale_e,
    inc,
    hid_n,
    pre_n,
    norm_n,
    scale_n,
    node_o,
    edge_o,
    send_buf,
    d_node,
    d_edge,
    d_node_f,
    d_edge_f,
    d_node_h,
    d_edge_h,
    halo_back,
    ret,
    cot_pe,
    cot_le,
    cot_pn,
    cot_ln,
    vec_acc,
    grad_half,
    grad_sib,
    sum_a,
    sum_b,
    recv_a1,
    recv_b1,
    half_a,
    half_b,
    recv_a2,
    recv_b2,
    fin,
    fin_sib,
    sem_local,
    sem_relay,
    sem_halo,
    sem_pair,
    sem_y,
    sem_z,
):
    seg = lax.axis_index("segment")
    dom = lax.axis_index("dom")
    core = lax.axis_index("dp")
    zed = dom // NY
    why = dom % NY
    first = seg == 0
    last = seg == SECTIONS - 1
    ahead = lax.rem(seg + 1, SECTIONS)
    behind = lax.rem(seg + SECTIONS - 1, SECTIONS)
    dom_next = lax.rem(dom + 1, DOMS)
    dom_prev = lax.rem(dom + DOMS - 1, DOMS)
    y_peers = [(seg, zed * NY + lax.rem(why + k, NY), core) for k in range(1, NY)]
    z_peers = [(seg, lax.rem(zed + k, NZ) * NY + why, core) for k in range(1, NZ)]
    sibling = (seg, dom, 1 - core)

    barrier = pltpu.get_barrier_semaphore()
    peers = y_peers + z_peers + [
        sibling,
        (ahead, dom, core),
        (behind, dom, core),
        (seg, dom_next, core),
        (seg, dom_prev, core),
    ]
    for peer in peers:
        pl.semaphore_signal(barrier, inc=1, device_id=peer, device_id_type=MESH)

    def local_copy(source, target, index):
        return pltpu.make_async_copy(source, target, sem_local.at[index])

    def span(sample):
        return pl.ds(sample * ROWS, ROWS)

    loads = [
        local_copy(w1e_hbm.at[0], w1e, 0),
        local_copy(w2e_hbm.at[0], w2e, 1),
        local_copy(w1n_hbm.at[0], w1n, 2),
        local_copy(w2n_hbm.at[0], w2n, 3),
    ]
    starts = []
    finals = []
    for sample in range(SAMPLES):
        starts.append(
            local_copy(node_in.at[sample], table.at[pl.ds(sample * 256, ROWS)], 4 + sample)
        )
        starts.append(local_copy(edge_in.at[sample], edge_x.at[span(sample)], 6 + sample))
        finals.append(local_copy(node_cot.at[sample], d_node.at[span(sample)], 8 + sample))
        finals.append(local_copy(edge_cot.at[sample], d_edge.at[span(sample)], 10 + sample))

    @pl.when(first)
    def _():
        for copy in starts:
            copy.start()

    for copy in loads:
        copy.start()

    @pl.when(last)
    def _():
        for copy in finals:
            copy.start()

    slots = lax.broadcasted_iota(jnp.int32, (2 * ROWS, ROWS), 0)
    own = slots[:ROWS]
    send_t = (own == send_rows[...]).astype(F32)
    recv_t = (own == receiver_row[...]).astype(F32)
    pick_t = (slots == sender_row[...]).astype(F32)
    send_pick = send_t.T.astype(BF16)
    recv_pick = recv_t.T.astype(BF16)
    sender_pick = pick_t.T.astype(BF16)
    send_t = send_t.astype(BF16)
    recv_t = recv_t.astype(BF16)
    pick_t = pick_t.astype(BF16)
    live = (lax.broadcasted_iota(jnp.int32, (ROWS, 1), 0) < edge_count[0]).astype(F32)
    coeffs[...] = vectors[...].astype(F32)

    def coeff(row):
        return coeffs[row : row + 1, :]

    def remote(source, target, sems, index, peer):
        return pltpu.make_async_remote_copy(
            src_ref=source,
            dst_ref=target,
            send_sem=sems.at[0, index],
            recv_sem=sems.at[1, index],
            device_id=peer,
            device_id_type=MESH,
        )

    def halo_copies(source, sample, target_ref, base, kind):
        return (
            remote(
                source.at[pl.ds(sample * ROWS, HALO)],
                target_ref.at[pl.ds(base + HALO, HALO)],
                sem_halo,
                kind * 4 + sample * 2,
                (seg, dom_prev, core),
            ),
            remote(
                source.at[pl.ds(sample * ROWS + HALO, HALO)],
                target_ref.at[pl.ds(base, HALO)],
                sem_halo,
                kind * 4 + sample * 2 + 1,
                (seg, dom_next, core),
            ),
        )

    def out_halo(sample):
        return halo_copies(send_buf, sample, table, sample * 256 + ROWS, 0)

    def back_halo(sample):
        return halo_copies(halo_back, sample, ret, sample * ROWS, 1)

    def node_relay(sample):
        return remote(
            node_o.at[span(sample)],
            table.at[pl.ds(sample * 256, ROWS)],
            sem_relay,
            sample,
            (ahead, dom, core),
        )

    def edge_relay(sample):
        return remote(
            edge_o.at[span(sample)],
            edge_x.at[span(sample)],
            sem_relay,
            2 + sample,
            (ahead, dom, core),
        )

    def node_return(sample):
        return remote(
            d_node_h.at[span(sample)],
            d_node.at[span(sample)],
            sem_relay,
            4 + sample,
            (behind, dom, core),
        )

    def edge_return(sample):
        return remote(
            d_edge_h.at[span(sample)],
            d_edge.at[span(sample)],
            sem_relay,
            6 + sample,
            (behind, dom, core),
        )

    def outputs(sample):
        return (
            local_copy(node_o.at[span(sample)], node_out.at[0, sample], 12 + sample),
            local_copy(edge_o.at[span(sample)], edge_out.at[0, sample], 14 + sample),
            local_copy(d_node_f.at[span(sample)], node_grad.at[0, sample], 16 + sample),
            local_copy(d_edge_f.at[span(sample)], edge_grad.at[0, sample], 18 + sample),
        )

    pl.semaphore_wait(barrier, len(peers))

    for sample in range(SAMPLES):
        rows = span(sample)
        own_rows = pl.ds(sample * 256, ROWS)

        @pl.when(first)
        def _():
            starts[2 * sample].wait()

        @pl.when(jnp.logical_not(first))
        def _():
            node_relay(sample).wait_recv()

        nodes = table[own_rows, :]
        node_x[rows, :] = nodes
        send_buf[rows, :] = dot_nn(send_pick, nodes).astype(BF16)
        for copy in out_halo(sample):
            copy.start()
        receivers = dot_nn(recv_pick, nodes).astype(BF16)
        rcv[rows, :] = receivers
        if sample == 0:
            for copy in loads:
                copy.wait()
        node_part = dot_nn(nodes, w1n[:D, :]) + coeff(4)
        edge_part = dot_nn(receivers, w1e[2 * D :, :]) + coeff(0)

        @pl.when(first)
        def _():
            starts[2 * sample + 1].wait()

        @pl.when(jnp.logical_not(first))
        def _():
            edge_relay(sample).wait_recv()

        edges = edge_x[rows, :]
        edge_part = edge_part + dot_nn(edges, w1e[:D, :])
        for copy in out_halo(sample):
            copy.wait_recv()
        senders = dot_nn(sender_pick, table[pl.ds(sample * 256, 256), :]).astype(BF16)
        snd[rows, :] = senders
        edge_pre = edge_part + dot_nn(senders, w1e[D : 2 * D, :])
        edge_hid = (edge_pre * sigmoid(edge_pre)).astype(BF16)
        pre_e[rows, :] = edge_pre
        hid_e[rows, :] = edge_hid
        edge_norm, edge_scale = norm_parts(dot_nn(edge_hid, w2e[...]) + coeff(1))
        norm_e[rows, :] = edge_norm
        scale_e[rows, :] = jnp.broadcast_to(edge_scale, (ROWS, 128))
        message = (edge_norm * coeff(2) + coeff(3)) * live
        edge_o[rows, :] = (edges.astype(F32) + message).astype(BF16)

        @pl.when(jnp.logical_not(last))
        def _():
            edge_relay(sample).start()

        incoming = dot_nn(recv_t, message.astype(BF16)).astype(BF16)
        inc[rows, :] = incoming
        node_pre = node_part + dot_nn(incoming, w1n[D:, :])
        node_hid = (node_pre * sigmoid(node_pre)).astype(BF16)
        pre_n[rows, :] = node_pre
        hid_n[rows, :] = node_hid
        node_norm, node_scale = norm_parts(dot_nn(node_hid, w2n[...]) + coeff(5))
        norm_n[rows, :] = node_norm
        scale_n[rows, :] = jnp.broadcast_to(node_scale, (ROWS, 128))
        node_o[rows, :] = (
            nodes.astype(F32) + node_norm * coeff(6) + coeff(7)
        ).astype(BF16)

        @pl.when(jnp.logical_not(last))
        def _():
            node_relay(sample).start()

        for copy in outputs(sample)[:2]:
            copy.start()

    def silu_slope(values):
        gate = sigmoid(values)
        return gate * (1.0 + values * (1.0 - gate))

    for sample in range(SAMPLES):
        rows = span(sample)

        @pl.when(last)
        def _():
            finals[2 * sample].wait()

        @pl.when(jnp.logical_not(last))
        def _():
            node_return(sample).wait_recv()

        node_back = d_node[rows, :].astype(F32)
        node_norm = norm_n[rows, :]
        node_lin_back = norm_back(node_back * coeff(6), node_norm, scale_n[rows, 0:1])
        lin_half = node_lin_back.astype(BF16)
        cot_ln[rows, :] = lin_half
        node_pre_back = dot_nt(lin_half, w2n[...]).astype(BF16).astype(F32) * silu_slope(
            pre_n[rows, :]
        )
        pre_half = node_pre_back.astype(BF16)
        cot_pn[rows, :] = pre_half
        node_total = node_back + dot_nt(pre_half, w1n[:D, :]).astype(BF16).astype(F32)
        incoming_back = dot_nt(pre_half, w1n[D:, :]).astype(BF16)

        @pl.when(last)
        def _():
            finals[2 * sample + 1].wait()

        @pl.when(jnp.logical_not(last))
        def _():
            edge_return(sample).wait_recv()

        edge_back = d_edge[rows, :].astype(F32)
        edge_norm = norm_e[rows, :]
        message_back = (edge_back + dot_nn(recv_pick, incoming_back)) * live
        edge_lin_back = norm_back(message_back * coeff(2), edge_norm, scale_e[rows, 0:1])
        lin_half = edge_lin_back.astype(BF16)
        cot_le[rows, :] = lin_half
        edge_pre_back = dot_nt(lin_half, w2e[...]).astype(BF16).astype(F32) * silu_slope(
            pre_e[rows, :]
        )
        pre_half = edge_pre_back.astype(BF16)
        cot_pe[rows, :] = pre_half
        sender_back = dot_nt(pre_half, w1e[D : 2 * D, :]).astype(BF16)
        halo_back[rows, :] = dot_nn(pick_t[ROWS:, :], sender_back).astype(BF16)
        for copy in back_halo(sample):
            copy.start()
        edge_total = edge_back + dot_nt(pre_half, w1e[:D, :]).astype(BF16).astype(F32)
        d_edge_f[rows, :] = edge_total
        d_edge_h[rows, :] = edge_total.astype(BF16)

        @pl.when(jnp.logical_not(first))
        def _():
            edge_return(sample).start()

        receiver_back = dot_nt(pre_half, w1e[2 * D :, :]).astype(BF16)
        node_total = node_total + dot_nn(pick_t[:ROWS, :], sender_back).astype(BF16).astype(F32)
        node_total = node_total + dot_nn(recv_t, receiver_back).astype(BF16).astype(F32)
        sums = (
            edge_pre_back,
            edge_lin_back,
            message_back * edge_norm,
            message_back,
            node_pre_back,
            node_lin_back,
            node_back * node_norm,
            node_back,
        )
        for index, value in enumerate(sums):
            vec_acc[sample, index : index + 1, :] = column_sum(value)
        for copy in back_halo(sample):
            copy.wait_recv()
        node_total = node_total + dot_nn(send_t, ret[rows, :])
        d_node_f[rows, :] = node_total
        d_node_h[rows, :] = node_total.astype(BF16)

        @pl.when(jnp.logical_not(first))
        def _():
            node_return(sample).start()

        for copy in outputs(sample)[2:]:
            copy.start()

    def put(start, value):
        width = value.shape[1]
        here = value.astype(BF16)
        if start >= HALF:
            grad_half[1, :, start - HALF : start - HALF + width] = here
        elif start + width <= HALF:
            grad_half[0, :, start : start + width] = here
        else:
            cut = HALF - start
            grad_half[0, :, start:HALF] = here[:, :cut]
            grad_half[1, :, 0 : width - cut] = here[:, cut:]

    edge_pre_t = cot_pe[...].T
    put(0, dot_nn(edge_pre_t, edge_x[...]))
    put(D, dot_nn(edge_pre_t, snd[...]))
    put(2 * D, dot_nn(edge_pre_t, rcv[...]))
    put(3 * D, dot_nn(cot_le[...].T, hid_e[...]))
    node_pre_t = cot_pn[...].T
    put(4 * D, dot_nn(node_pre_t, node_x[...]))
    put(5 * D, dot_nn(node_pre_t, inc[...]))
    put(6 * D, dot_nn(cot_ln[...].T, hid_n[...]))
    vec_sum = vec_acc[0] + vec_acc[1]
    vec_block = jnp.concatenate([vec_sum, jnp.zeros((120, D), F32)], 0).T
    put(7 * D, jnp.concatenate([vec_block, jnp.zeros((D, 128), F32)], 1))

    pair = remote(grad_half.at[1 - core], grad_sib, sem_pair, 0, sibling)
    pair.start()
    pair.wait()
    for z_at in range(NZ):
        here = pl.ds(z_at * NY * 16, NY * 16)
        total = grad_half[core, here, :].astype(F32) + grad_sib[here, :].astype(F32)
        total = total.astype(BF16).reshape(NY, 16, HALF)
        sum_a[z_at] = total[:, :, :LANES_A]
        sum_b[z_at] = total[:, :, LANES_A:]

    copies = []
    for k in range(1, NY):
        target = lax.rem(why + k, NY)
        copies.append(
            remote(sum_a.at[:, target], recv_a1.at[k - 1], sem_y, k - 1, y_peers[k - 1])
        )
    for k in range(1, NZ):
        target = lax.rem(zed + k, NZ)
        copies.append(
            remote(sum_b.at[target], recv_b1.at[k - 1], sem_z, k - 1, z_peers[k - 1])
        )
    for copy in copies:
        copy.start()
    for copy in copies[: NY - 1]:
        copy.wait_recv()
    for z_at in range(NZ):
        total = sum_a[z_at, why].astype(F32)
        for k in range(NY - 1):
            total = total + recv_a1[k, z_at].astype(F32)
        half_a[z_at] = total.astype(BF16)
    copies_2 = []
    for k in range(1, NZ):
        target = lax.rem(zed + k, NZ)
        copies_2.append(
            remote(half_a.at[target], recv_a2.at[k - 1], sem_z, NZ - 2 + k, z_peers[k - 1])
        )
    for copy in copies_2:
        copy.start()
    for copy in copies[NY - 1 :]:
        copy.wait_recv()
    for y_at in range(NY):
        total = sum_b[zed, y_at].astype(F32)
        for k in range(NZ - 1):
            total = total + recv_b1[k, y_at].astype(F32)
        half_b[y_at] = total.astype(BF16)
    copies_3 = []
    for k in range(1, NY):
        target = lax.rem(why + k, NY)
        copies_3.append(
            remote(half_b.at[target], recv_b2.at[k - 1], sem_y, NY - 2 + k, y_peers[k - 1])
        )
    for copy in copies_3:
        copy.start()
    for copy in copies_2:
        copy.wait_recv()
    total = half_a[zed].astype(F32)
    for k in range(NZ - 1):
        total = total + recv_a2[k].astype(F32)
    fin[0, :, :LANES_A] = total[:8]
    fin[1, :, :LANES_A] = total[8:]
    for copy in copies_3:
        copy.wait_recv()
    total = half_b[why].astype(F32)
    for k in range(NY - 1):
        total = total + recv_b2[k].astype(F32)
    fin[0, :, LANES_A:] = total[:8]
    fin[1, :, LANES_A:] = total[8:]
    swap = remote(fin.at[1 - core], fin_sib, sem_pair, 1, sibling)
    swap.start()
    swap.wait_recv()
    grads_out[core] = fin[core]
    grads_out[1 - core] = fin_sib[...]

    swap.wait_send()
    for copy in copies + copies_2 + copies_3:
        copy.wait_send()
    for sample in range(SAMPLES):
        for copy in out_halo(sample) + back_halo(sample):
            copy.wait_send()
        for copy in outputs(sample):
            copy.wait()

        @pl.when(jnp.logical_not(last))
        def _():
            edge_relay(sample).wait_send()
            node_relay(sample).wait_send()

        @pl.when(jnp.logical_not(first))
        def _():
            edge_return(sample).wait_send()
            node_return(sample).wait_send()


def local(
    node_in,
    edge_in,
    node_cot,
    edge_cot,
    send_rows,
    sender_row,
    receiver_row,
    edge_count,
    edge_w1,
    edge_w2,
    node_w1,
    node_w2,
    vectors,
):
    anywhere = pl.BlockSpec(memory_space=pl.ANY)
    vmem = pl.BlockSpec(memory_space=pltpu.VMEM)
    smem = pl.BlockSpec(memory_space=pltpu.SMEM)
    both = SAMPLES * ROWS

    def half(*shape):
        return pltpu.VMEM(shape, BF16)

    def full(*shape):
        return pltpu.VMEM(shape, F32)

    scratch = [
        half(3 * D, D),
        half(D, D),
        half(2 * D, D),
        half(D, D),
        full(8, D),
        half(2 * both, D),
        half(both, D),
        half(both, D),
        half(both, D),
        half(both, D),
        half(both, D),
        full(both, D),
        full(both, D),
        full(both, 128),
        half(both, D),
        half(both, D),
        full(both, D),
        full(both, D),
        full(both, 128),
        half(both, D),
        half(both, D),
        half(both, D),
        half(both, D),
        half(both, D),
        full(both, D),
        full(both, D),
        half(both, D),
        half(both, D),
        half(both, D),
        half(both, D),
        half(both, D),
        half(both, D),
        half(both, D),
        half(both, D),
        full(SAMPLES, 8, D),
        half(2, D, HALF),
        half(D, HALF),
        half(NZ, NY, 16, LANES_A),
        half(NZ, NY, 16, LANES_B),
        half(NY - 1, NZ, 16, LANES_A),
        half(NZ - 1, NY, 16, LANES_B),
        half(NZ, 16, LANES_A),
        half(NY, 16, LANES_B),
        half(NZ - 1, 16, LANES_A),
        half(NY - 1, 16, LANES_B),
        full(2, 8, HALF),
        full(8, HALF),
        pltpu.SemaphoreType.DMA((20,)),
        pltpu.SemaphoreType.DMA((2, 8)),
        pltpu.SemaphoreType.DMA((2, 8)),
        pltpu.SemaphoreType.DMA((2, 2)),
        pltpu.SemaphoreType.DMA((2, 6)),
        pltpu.SemaphoreType.DMA((2, 14)),
    ]
    shape = (1, SAMPLES, ROWS, D)
    node_out, edge_out, node_grad, edge_grad, grads = pl.pallas_call(
        kernel,
        out_shape=(
            jax.ShapeDtypeStruct(shape, BF16),
            jax.ShapeDtypeStruct(shape, BF16),
            jax.ShapeDtypeStruct(shape, F32),
            jax.ShapeDtypeStruct(shape, F32),
            jax.ShapeDtypeStruct((2, 8, HALF), F32),
        ),
        in_specs=[anywhere] * 4 + [vmem] * 3 + [smem] + [anywhere] * 4 + [vmem],
        out_specs=(anywhere,) * 4 + (vmem,),
        scratch_shapes=scratch,
        compiler_params=pltpu.CompilerParams(
            collective_id=0, has_side_effects=True, vmem_limit_bytes=48 << 20
        ),
        name="layers",
    )(
        node_in,
        edge_in,
        node_cot,
        edge_cot,
        send_rows.reshape(1, ROWS),
        sender_row.reshape(1, ROWS),
        receiver_row.reshape(1, ROWS),
        edge_count,
        edge_w1,
        edge_w2,
        node_w1,
        node_w2,
        vectors[0],
    )
    columns = jnp.concatenate([grads[0], grads[1]], 1).T
    return (
        node_out,
        edge_out,
        node_grad,
        edge_grad,
        columns[None, : 3 * D],
        columns[None, 3 * D : 4 * D],
        columns[None, 4 * D : 6 * D],
        columns[None, 6 * D : 7 * D],
        columns[None, 7 * D : 7 * D + 8],
    )


def solution(mesh):
    in_specs = (
        P("dp", "dom", None),
        P("dp", "dom", None),
        P("dp", "dom", None),
        P("dp", "dom", None),
        P("dom"),
        P("dom"),
        P("dom"),
        P("dom"),
        P("segment", None, None),
        P("segment", None, None),
        P("segment", None, None),
        P("segment", None, None),
        P("segment", None, None),
    )
    out_specs = (
        P("segment", "dp", "dom", None),
        P("segment", "dp", "dom", None),
        P("segment", "dp", "dom", None),
        P("segment", "dp", "dom", None),
        P("segment", None, ("dom", "dp")),
        P("segment", None, ("dom", "dp")),
        P("segment", None, ("dom", "dp")),
        P("segment", None, ("dom", "dp")),
        P("segment", None, ("dom", "dp")),
    )
    return jax.shard_map(local, mesh=mesh, in_specs=in_specs, out_specs=out_specs, check_vma=False)
```

time: 726 us -> 157 us (0.22); the launches traced: 713 us -> 156 us
  blocking collectives: 253 us -> 0 us
  Pallas kernels: 0 us -> 140 us
  starting transfers between devices: 115 us -> 0 us
  other arithmetic: 102 us -> 0.01 us
  local copies, waits for them, and re-layouts: 112 us -> 15.3 us
  waiting for transfers between devices: 71.6 us -> 0 us
  matrix products: 39.9 us -> 0 us
  between operations: 18.5 us -> 1.35 us
    unnamed x1 -> x0, blocking collectives: 253 us -> none
    pallas_call x0 -> x1, Pallas kernels: none -> 140 us  [local(): pl.pallas_call(kernel, out_shape=(jax.ShapeDtypeStruct(shape, BF16), jax....]
    ppermute x36 -> x0, starting transfers between devices: 115 us -> none  [the longest x16 62.5 us: passed_along(): lax.ppermute(value, axis, [(source, source + steps) for source in range(i...]
    ppermute x36 -> x0, waiting for transfers between devices: 71.6 us -> none  [the longest x16 71.5 us: passed_along(): lax.ppermute(value, axis, [(source, source + steps) for source in range(i...]
    dynamic_slice x67 -> x0, local copies, waits for them, and re-layouts: 57 us -> none  [keep_slot(): current = lax.dynamic_index_in_dim(buffer, keep_index, 0, keepdims=False)]
    dynamic_update_slice x95 -> x0, other arithmetic: 54.6 us -> none  [keep_slot(): lax.dynamic_update_index_in_dim(buffer, jnp.where(active, value, current)...]
    dot_general x42 -> x0, matrix products: 39.9 us -> none  [the longest x6 7.65 us: layer_local(): jnp.dot(edge_hid, edge_w2, preferred_element_type=jnp.float32) + coeffs[1]]
    scatter-add x5 -> x0, other arithmetic: 15.2 us -> none  [local(): jnp.zeros_like(node_back).at[send_rows].add(arrived(returned, margin))]
  transfers between devices with their start and end apart: 37 -> 0, of which waited for: 7 -> 0; matrix products, arithmetic and copies ran while one was open for 21% -> 0% of each run, Pallas kernels for 0% -> 0%
where the time goes in v1:
time: 157 us; the launch traced here: 156 us
  Pallas kernels  140 us (89%)
  local copies, waits for them, and re-layouts  15.3 us (10%)
    pallas_call x1, Pallas kernels, local(): pl.pallas_call(kernel, out_shape=(jax.ShapeDtypeStruct(shape, BF16), jax....  140 us
    unnamed x26, local copies, waits for them, and re-layouts  12.7 us

profile of v1, /device:TPU:1, one launch (start us, length us, event | category | flops | bytes accessed | tf_op | source)
XLA Modules:
  0.0 156.3 jit_solution(16601757823829722095)
XLA Ops:
  1.3 0.0 copy-start
  1.3 1.2 copy-done
  2.5 0.0 copy-start.1
  2.5 1.0 copy-done.1
  3.6 0.0 copy-start.2
  3.6 1.0 copy-done.2
  4.6 0.0 copy-start.3
  4.6 0.9 copy-done.3
  5.6 0.0 copy-start.4
  5.6 0.9 copy-done.4
  6.5 0.0 copy-start.5
  6.5 0.9 copy-done.5
  7.5 0.0 copy-start.6
  7.5 0.9 copy-done.6
  8.4 0.0 copy-start.7
  8.4 0.7 copy-done.7
  9.1 0.0 copy-start.8
  9.1 0.7 copy-done.8
  9.8 0.0 copy-start.9
  9.8 0.7 copy-done.9
  10.4 0.0 copy-start.10
  10.4 0.7 copy-done.10
  11.1 139.6 %layers.1 = (bf16[1,2,128,512]{3,2,1,0:T(8,128)(2,1)S(1)}, bf16[1,2,128,512]{3,2,1,0:T(8,128)(2,1)S(1)}, f32[1,2,128,512]{3,2,1,0:T(8,128)S(1)}, f32[1,2,128,512]{3,2,1,0:T(8,128)S(1)}, f32[2,8,1920]{2,1,0:T(8,128)S(1)}) custom-call(bf16[2,128,512]{2,1,0:T(8,128)(2,1)S(1)} %copy-done.3, bf16[2,128,512]{2,1,0:T(8,128)(2,1)S(1)} %copy-done.4, ...), custom_call_target="tpu_custom_call" | custom-call | tf_op jit(solution)/shard_map/layers/pallas_call | solution.py:647
  150.8 0.7 copy.22
  151.4 0.6 slice_bitcast_fusion.3
  152.0 0.6 slice_bitcast_fusion.4
  152.7 0.6 slice_bitcast_fusion.2
  153.3 0.7 copy.28
  154.0 0.7 copy.29
  154.7 0.8 copy.30
  155.5 0.8 copy.31
  (3 shorter events, 0.0 us)
Async XLA Ops:
  1.3 1.2 copy-start
  2.5 1.0 copy-start.1
  3.6 1.0 copy-start.2
  4.6 0.9 copy-start.3
  5.6 0.9 copy-start.4
  6.5 0.9 copy-start.5
  7.5 0.9 copy-start.6
  8.4 0.7 copy-start.7
  9.1 0.7 copy-start.8
  9.8 0.7 copy-start.9
  10.4 0.7 copy-start.10

commit v2 on v1

--- a/solution.py
+++ b/solution.py
@@ -22,6 +22,8 @@
 HALF = 1920
 LANES_A = 1280
 LANES_B = HALF - LANES_A
+CUT_A = 640
+CUT_B = 384
 
 
 def dot_nn(left, right):
@@ -58,15 +60,15 @@
     edge_in,
     node_cot,
     edge_cot,
-    send_rows,
-    sender_row,
-    receiver_row,
+    send_rows_hbm,
+    sender_row_hbm,
+    receiver_row_hbm,
     edge_count,
     w1e_hbm,
     w2e_hbm,
     w1n_hbm,
     w2n_hbm,
-    vectors,
+    vectors_hbm,
     node_out,
     edge_out,
     node_grad,
@@ -76,6 +78,10 @@
     w2e,
     w1n,
     w2n,
+    send_rows,
+    sender_row,
+    receiver_row,
+    vectors,
     coeffs,
     table,
     edge_x,
@@ -111,12 +117,12 @@
     grad_sib,
     sum_a,
     sum_b,
-    recv_a1,
-    recv_b1,
     half_a,
     half_b,
-    recv_a2,
-    recv_b2,
+    fold_ay,
+    fold_bz,
+    fold_az,
+    fold_by,
     fin,
     fin_sib,
     sem_local,
@@ -137,12 +143,20 @@
     behind = lax.rem(seg + SECTIONS - 1, SECTIONS)
     dom_next = lax.rem(dom + 1, DOMS)
     dom_prev = lax.rem(dom + DOMS - 1, DOMS)
-    y_peers = [(seg, zed * NY + lax.rem(why + k, NY), core) for k in range(1, NY)]
-    z_peers = [(seg, lax.rem(zed + k, NZ) * NY + why, core) for k in range(1, NZ)]
+    y_at = [lax.rem(why + k, NY) for k in range(NY)]
+    z_at = [lax.rem(zed + k, NZ) for k in range(NZ)]
+    y_peer = [(seg, zed * NY + at, core) for at in y_at]
+    z_peer = [(seg, at * NY + why, core) for at in z_at]
     sibling = (seg, dom, 1 - core)
 
     barrier = pltpu.get_barrier_semaphore()
-    peers = y_peers + z_peers + [
+    peers = [
+        y_peer[1],
+        y_peer[3],
+        z_peer[1],
+        z_peer[2],
+        z_peer[6],
+        z_peer[7],
         sibling,
         (ahead, dom, core),
         (behind, dom, core),
@@ -164,6 +178,12 @@
         local_copy(w1n_hbm.at[0], w1n, 2),
         local_copy(w2n_hbm.at[0], w2n, 3),
     ]
+    lists = [
+        local_copy(send_rows_hbm, send_rows, 20),
+        local_copy(sender_row_hbm, sender_row, 21),
+        local_copy(receiver_row_hbm, receiver_row, 22),
+        local_copy(vectors_hbm.at[0], vectors, 23),
+    ]
     starts = []
     finals = []
     for sample in range(SAMPLES):
@@ -174,6 +194,9 @@
         finals.append(local_copy(node_cot.at[sample], d_node.at[span(sample)], 8 + sample))
         finals.append(local_copy(edge_cot.at[sample], d_edge.at[span(sample)], 10 + sample))
 
+    for copy in lists:
+        copy.start()
+
     @pl.when(first)
     def _():
         for copy in starts:
@@ -187,6 +210,8 @@
         for copy in finals:
             copy.start()
 
+    for copy in lists:
+        copy.wait()
     slots = lax.broadcasted_iota(jnp.int32, (2 * ROWS, ROWS), 0)
     own = slots[:ROWS]
     send_t = (own == send_rows[...]).astype(F32)
@@ -278,34 +303,43 @@
         return (
             local_copy(node_o.at[span(sample)], node_out.at[0, sample], 12 + sample),
             local_copy(edge_o.at[span(sample)], edge_out.at[0, sample], 14 + sample),
+        )
+
+    def grad_outputs(sample):
+        return (
             local_copy(d_node_f.at[span(sample)], node_grad.at[0, sample], 16 + sample),
             local_copy(d_edge_f.at[span(sample)], edge_grad.at[0, sample], 18 + sample),
         )
 
     pl.semaphore_wait(barrier, len(peers))
 
+    def gather(sample):
+        nodes = table[pl.ds(sample * 256, ROWS), :]
+        send_buf[span(sample), :] = dot_nn(send_pick, nodes).astype(BF16)
+        for copy in out_halo(sample):
+            copy.start()
+        node_x[span(sample), :] = nodes
+
+    @pl.when(first)
+    def _():
+        for sample in range(SAMPLES):
+            starts[2 * sample].wait()
+            gather(sample)
+
     for sample in range(SAMPLES):
         rows = span(sample)
-        own_rows = pl.ds(sample * 256, ROWS)
-
-        @pl.when(first)
-        def _():
-            starts[2 * sample].wait()
-
-        @pl.when(jnp.logical_not(first))
-        def _():
-            node_relay(sample).wait_recv()
-
-        nodes = table[own_rows, :]
-        node_x[rows, :] = nodes
-        send_buf[rows, :] = dot_nn(send_pick, nodes).astype(BF16)
-        for copy in out_halo(sample):
-            copy.start()
+        if sample == 0:
+
+            @pl.when(jnp.logical_not(first))
+            def _():
+                node_relay(0).wait_recv()
+                gather(0)
+
+            for copy in loads:
+                copy.wait()
+        nodes = node_x[rows, :]
         receivers = dot_nn(recv_pick, nodes).astype(BF16)
         rcv[rows, :] = receivers
-        if sample == 0:
-            for copy in loads:
-                copy.wait()
         node_part = dot_nn(nodes, w1n[:D, :]) + coeff(4)
         edge_part = dot_nn(receivers, w1e[2 * D :, :]) + coeff(0)
 
@@ -332,10 +366,16 @@
         scale_e[rows, :] = jnp.broadcast_to(edge_scale, (ROWS, 128))
         message = (edge_norm * coeff(2) + coeff(3)) * live
         edge_o[rows, :] = (edges.astype(F32) + message).astype(BF16)
-
-        @pl.when(jnp.logical_not(last))
-        def _():
-            edge_relay(sample).start()
+        if sample == 0:
+
+            @pl.when(jnp.logical_not(last))
+            def _():
+                edge_relay(0).start()
+
+            @pl.when(jnp.logical_not(first))
+            def _():
+                node_relay(1).wait_recv()
+                gather(1)
 
         incoming = dot_nn(recv_t, message.astype(BF16)).astype(BF16)
         inc[rows, :] = incoming
@@ -346,15 +386,15 @@
         node_norm, node_scale = norm_parts(dot_nn(node_hid, w2n[...]) + coeff(5))
         norm_n[rows, :] = node_norm
         scale_n[rows, :] = jnp.broadcast_to(node_scale, (ROWS, 128))
-        node_o[rows, :] = (
-            nodes.astype(F32) + node_norm * coeff(6) + coeff(7)
-        ).astype(BF16)
+        node_o[rows, :] = (nodes.astype(F32) + node_norm * coeff(6) + coeff(7)).astype(BF16)
 
         @pl.when(jnp.logical_not(last))
         def _():
             node_relay(sample).start()
-
-        for copy in outputs(sample)[:2]:
+            if sample == 1:
+                edge_relay(1).start()
+
+        for copy in outputs(sample):
             copy.start()
 
     def silu_slope(values):
@@ -431,18 +471,7 @@
         )
         for index, value in enumerate(sums):
             vec_acc[sample, index : index + 1, :] = column_sum(value)
-        for copy in back_halo(sample):
-            copy.wait_recv()
-        node_total = node_total + dot_nn(send_t, ret[rows, :])
         d_node_f[rows, :] = node_total
-        d_node_h[rows, :] = node_total.astype(BF16)
-
-        @pl.when(jnp.logical_not(first))
-        def _():
-            node_return(sample).start()
-
-        for copy in outputs(sample)[2:]:
-            copy.start()
 
     def put(start, value):
         width = value.shape[1]
@@ -471,71 +500,144 @@
 
     pair = remote(grad_half.at[1 - core], grad_sib, sem_pair, 0, sibling)
     pair.start()
+    for sample in range(SAMPLES):
+        rows = span(sample)
+        for copy in back_halo(sample):
+            copy.wait_recv()
+        node_total = d_node_f[rows, :] + dot_nn(send_t, ret[rows, :])
+        d_node_f[rows, :] = node_total
+        d_node_h[rows, :] = node_total.astype(BF16)
+
+        @pl.when(jnp.logical_not(first))
+        def _():
+            node_return(sample).start()
+
+        for copy in grad_outputs(sample):
+            copy.start()
+
     pair.wait()
-    for z_at in range(NZ):
-        here = pl.ds(z_at * NY * 16, NY * 16)
+    for at in range(NZ):
+        here = pl.ds(at * NY * 16, NY * 16)
         total = grad_half[core, here, :].astype(F32) + grad_sib[here, :].astype(F32)
         total = total.astype(BF16).reshape(NY, 16, HALF)
-        sum_a[z_at] = total[:, :, :LANES_A]
-        sum_b[z_at] = total[:, :, LANES_A:]
-
-    copies = []
-    for k in range(1, NY):
-        target = lax.rem(why + k, NY)
-        copies.append(
-            remote(sum_a.at[:, target], recv_a1.at[k - 1], sem_y, k - 1, y_peers[k - 1])
-        )
-    for k in range(1, NZ):
-        target = lax.rem(zed + k, NZ)
-        copies.append(
-            remote(sum_b.at[target], recv_b1.at[k - 1], sem_z, k - 1, z_peers[k - 1])
-        )
-    for copy in copies:
-        copy.start()
-    for copy in copies[: NY - 1]:
-        copy.wait_recv()
-    for z_at in range(NZ):
-        total = sum_a[z_at, why].astype(F32)
-        for k in range(NY - 1):
-            total = total + recv_a1[k, z_at].astype(F32)
-        half_a[z_at] = total.astype(BF16)
-    copies_2 = []
-    for k in range(1, NZ):
-        target = lax.rem(zed + k, NZ)
-        copies_2.append(
-            remote(half_a.at[target], recv_a2.at[k - 1], sem_z, NZ - 2 + k, z_peers[k - 1])
-        )
-    for copy in copies_2:
-        copy.start()
-    for copy in copies[NY - 1 :]:
-        copy.wait_recv()
-    for y_at in range(NY):
-        total = sum_b[zed, y_at].astype(F32)
-        for k in range(NZ - 1):
-            total = total + recv_b1[k, y_at].astype(F32)
-        half_b[y_at] = total.astype(BF16)
-    copies_3 = []
-    for k in range(1, NY):
-        target = lax.rem(why + k, NY)
-        copies_3.append(
-            remote(half_b.at[target], recv_b2.at[k - 1], sem_y, NY - 2 + k, y_peers[k - 1])
-        )
-    for copy in copies_3:
-        copy.start()
-    for copy in copies_2:
-        copy.wait_recv()
-    total = half_a[zed].astype(F32)
-    for k in range(NZ - 1):
-        total = total + recv_a2[k].astype(F32)
+        sum_a[at] = total[:, :, :LANES_A]
+        sum_b[at] = total[:, :, LANES_A:]
+
+    def wide(ref):
+        return ref[...].astype(F32)
+
+    class YFold:
+        def __init__(self, source, load, cut, parts, base):
+            fold_p, fold_m, self.stage_p, self.stage_m, self.p0, self.p1, self.m0, self.m1 = parts
+            low, high = slice(0, cut), slice(cut, None)
+            self.load, self.low, self.high = load, low, high
+            self.fold_p, self.fold_m = fold_p, fold_m
+
+            def send(src, target, index, peer):
+                return remote(src, target, sem_y, base + index, y_peer[peer])
+
+            self.fp = send(source(y_at[2], low), fold_p, 0, 1)
+            self.fm = send(source(y_at[2], high), fold_m, 1, 3)
+            self.c_p1 = send(source(y_at[1], high), self.p1, 2, 1)
+            self.c_m0 = send(source(y_at[3], low), self.m0, 3, 3)
+            self.c_p0 = send(self.stage_p, self.p0, 4, 1)
+            self.c_m1 = send(self.stage_m, self.m1, 5, 3)
+            self.all = (self.fp, self.fm, self.c_p1, self.c_m0, self.c_p0, self.c_m1)
+
+        def start(self):
+            for copy in self.all[:4]:
+                copy.start()
+
+        def middle(self):
+            self.fp.wait_recv()
+            total = self.load(y_at[1], self.low).astype(F32) + wide(self.fold_p)
+            self.stage_p[...] = total.astype(BF16)
+            self.c_p0.start()
+            self.fm.wait_recv()
+            total = self.load(y_at[3], self.high).astype(F32) + wide(self.fold_m)
+            self.stage_m[...] = total.astype(BF16)
+            self.c_m1.start()
+
+        def finish(self):
+            for copy in self.all[2:]:
+                copy.wait_recv()
+            low = self.load(y_at[0], self.low).astype(F32) + wide(self.p0) + wide(self.m0)
+            high = self.load(y_at[0], self.high).astype(F32) + wide(self.p1) + wide(self.m1)
+            return low, high
+
+    class ZFold:
+        def __init__(self, source, cut, parts, base):
+            self.r4p, self.r4m, self.r3p, self.r3m, self.r1p, self.r1m = parts[:6]
+            self.stage_p, self.stage_m, self.r2p, self.r2m = parts[6:]
+            self.source, self.cut = source, cut
+
+            def send(src, target, index, peer):
+                return remote(src, target, sem_z, base + index, z_peer[peer])
+
+            far = source.at[z_at[4]]
+            self.all = (
+                send(far.at[..., :cut], self.r4p, 0, 2),
+                send(far.at[..., cut:], self.r4m, 1, 6),
+                send(source.at[z_at[3]], self.r3p, 2, 1),
+                send(source.at[z_at[5]], self.r3m, 3, 7),
+                send(source.at[z_at[1]], self.r1p, 4, 1),
+                send(source.at[z_at[7]], self.r1m, 5, 7),
+                send(self.stage_p, self.r2p, 6, 2),
+                send(self.stage_m, self.r2m, 7, 6),
+            )
+
+        def start(self):
+            for copy in self.all[:6]:
+                copy.start()
+
+        def middle(self):
+            cut = self.cut
+            self.all[2].wait_recv()
+            self.all[0].wait_recv()
+            total = self.source[z_at[2]].astype(F32) + wide(self.r3p)
+            self.stage_p[..., cut:] = total[..., cut:].astype(BF16)
+            self.stage_p[..., :cut] = (total[..., :cut] + wide(self.r4p)).astype(BF16)
+            self.all[6].start()
+            self.all[3].wait_recv()
+            self.all[1].wait_recv()
+            total = self.source[z_at[6]].astype(F32) + wide(self.r3m)
+            self.stage_m[..., :cut] = total[..., :cut].astype(BF16)
+            self.stage_m[..., cut:] = (total[..., cut:] + wide(self.r4m)).astype(BF16)
+            self.all[7].start()
+
+        def finish(self):
+            for copy in self.all[4:]:
+                copy.wait_recv()
+            total = self.source[z_at[0]].astype(F32) + wide(self.r1p) + wide(self.r1m)
+            return total + wide(self.r2p) + wide(self.r2m)
+
+    a_y = YFold(
+        lambda at, lanes: sum_a.at[:, at, :, lanes], lambda at, lanes: sum_a[:, at, :, lanes], CUT_A, fold_ay, 0
+    )
+    b_z = ZFold(sum_b, CUT_B, fold_bz, 0)
+    a_z = ZFold(half_a, CUT_A, fold_az, 8)
+    b_y = YFold(
+        lambda at, lanes: half_b.at[at, :, lanes], lambda at, lanes: half_b[at, :, lanes], CUT_B, fold_by, 6
+    )
+    a_y.start()
+    b_z.start()
+    b_z.middle()
+    a_y.middle()
+    half_b[...] = b_z.finish().astype(BF16)
+    b_y.start()
+    low, high = a_y.finish()
+    half_a[:, :, :CUT_A] = low.astype(BF16)
+    half_a[:, :, CUT_A:] = high.astype(BF16)
+    a_z.start()
+    b_y.middle()
+    low, high = b_y.finish()
+    for index, rows in enumerate((slice(0, 8), slice(8, 16))):
+        fin[index, :, LANES_A : LANES_A + CUT_B] = low[rows]
+        fin[index, :, LANES_A + CUT_B :] = high[rows]
+    a_z.middle()
+    total = a_z.finish()
     fin[0, :, :LANES_A] = total[:8]
     fin[1, :, :LANES_A] = total[8:]
-    for copy in copies_3:
-        copy.wait_recv()
-    total = half_b[why].astype(F32)
-    for k in range(NY - 1):
-        total = total + recv_b2[k].astype(F32)
-    fin[0, :, LANES_A:] = total[:8]
-    fin[1, :, LANES_A:] = total[8:]
     swap = remote(fin.at[1 - core], fin_sib, sem_pair, 1, sibling)
     swap.start()
     swap.wait_recv()
@@ -543,12 +645,12 @@
     grads_out[1 - core] = fin_sib[...]
 
     swap.wait_send()
-    for copy in copies + copies_2 + copies_3:
+    for copy in a_y.all + b_z.all + a_z.all + b_y.all:
         copy.wait_send()
     for sample in range(SAMPLES):
         for copy in out_halo(sample) + back_halo(sample):
             copy.wait_send()
-        for copy in outputs(sample):
+        for copy in outputs(sample) + grad_outputs(sample):
             copy.wait()
 
         @pl.when(jnp.logical_not(last))
@@ -560,6 +662,36 @@
         def _():
             edge_return(sample).wait_send()
             node_return(sample).wait_send()
+
+
+def store_kernel(node_out, edge_out, node_grad, edge_grad, grads, *refs):
+    results, held, rows_held, sems = refs[:9], refs[9:13], refs[13:18], refs[18]
+    sources = (node_out, edge_out, node_grad, edge_grad)
+    loads = [
+        pltpu.make_async_copy(source, target, sems.at[index])
+        for index, (source, target) in enumerate(zip(sources, held))
+    ]
+    stores = [
+        pltpu.make_async_copy(source, target, sems.at[4 + index])
+        for index, (source, target) in enumerate(zip(held + rows_held, results))
+    ]
+    for copy in loads:
+        copy.start()
+    w1e_rows, w2e_rows, w1n_rows, w2n_rows, vec_rows = rows_held
+    w1e_rows[:, :] = grads[0, :, : 3 * D]
+    w2e_rows[:, : HALF - 3 * D] = grads[0, :, 3 * D :]
+    w2e_rows[:, HALF - 3 * D :] = grads[1, :, : 4 * D - HALF]
+    w1n_rows[:, :] = grads[1, :, 4 * D - HALF : 6 * D - HALF]
+    w2n_rows[:, :] = grads[1, :, 6 * D - HALF : 7 * D - HALF]
+    columns = grads[1, :, 7 * D - HALF : 7 * D - HALF + 128].T
+    vec_rows[...] = columns[:8, :]
+    for copy in stores[4:]:
+        copy.start()
+    for load, copy in zip(loads, stores):
+        load.wait()
+        copy.start()
+    for copy in stores:
+        copy.wait()
 
 
 def local(
@@ -588,11 +720,22 @@
     def full(*shape):
         return pltpu.VMEM(shape, F32)
 
+    def y_parts(lead, lanes, cut):
+        low, high = half(*lead, cut), half(*lead, lanes - cut)
+        return [low, high, low, high, low, high, low, high]
+
+    def z_parts(lead, lanes, cut):
+        return [half(*lead, cut), half(*lead, lanes - cut)] + [half(*lead, lanes)] * 8
+
     scratch = [
         half(3 * D, D),
         half(D, D),
         half(2 * D, D),
         half(D, D),
+        pltpu.VMEM((1, ROWS), jnp.int32),
+        pltpu.VMEM((1, ROWS), jnp.int32),
+        pltpu.VMEM((1, ROWS), jnp.int32),
+        half(8, D),
         full(8, D),
         half(2 * both, D),
         half(both, D),
@@ -628,20 +771,20 @@
         half(D, HALF),
         half(NZ, NY, 16, LANES_A),
         half(NZ, NY, 16, LANES_B),
-        half(NY - 1, NZ, 16, LANES_A),
-        half(NZ - 1, NY, 16, LANES_B),
         half(NZ, 16, LANES_A),
         half(NY, 16, LANES_B),
-        half(NZ - 1, 16, LANES_A),
-        half(NY - 1, 16, LANES_B),
+        y_parts((NZ, 16), LANES_A, CUT_A),
+        z_parts((NY, 16), LANES_B, CUT_B),
+        z_parts((16,), LANES_A, CUT_A),
+        y_parts((16,), LANES_B, CUT_B),
         full(2, 8, HALF),
         full(8, HALF),
-        pltpu.SemaphoreType.DMA((20,)),
+        pltpu.SemaphoreType.DMA((24,)),
         pltpu.SemaphoreType.DMA((2, 8)),
         pltpu.SemaphoreType.DMA((2, 8)),
         pltpu.SemaphoreType.DMA((2, 2)),
-        pltpu.SemaphoreType.DMA((2, 6)),
-        pltpu.SemaphoreType.DMA((2, 14)),
+        pltpu.SemaphoreType.DMA((2, 12)),
+        pltpu.SemaphoreType.DMA((2, 16)),
     ]
     shape = (1, SAMPLES, ROWS, D)
     node_out, edge_out, node_grad, edge_grad, grads = pl.pallas_call(
@@ -653,11 +796,11 @@
             jax.ShapeDtypeStruct(shape, F32),
             jax.ShapeDtypeStruct((2, 8, HALF), F32),
         ),
-        in_specs=[anywhere] * 4 + [vmem] * 3 + [smem] + [anywhere] * 4 + [vmem],
+        in_specs=[anywhere] * 7 + [smem] + [anywhere] * 5,
         out_specs=(anywhere,) * 4 + (vmem,),
         scratch_shapes=scratch,
         compiler_params=pltpu.CompilerParams(
-            collective_id=0, has_side_effects=True, vmem_limit_bytes=48 << 20
+            collective_id=0, has_side_effects=True, vmem_limit_bytes=60 << 20
         ),
         name="layers",
     )(
@@ -673,20 +816,27 @@
         edge_w2,
         node_w1,
         node_w2,
-        vectors[0],
+        vectors,
     )
-    columns = jnp.concatenate([grads[0], grads[1]], 1).T
-    return (
-        node_out,
-        edge_out,
-        node_grad,
-        edge_grad,
-        columns[None, : 3 * D],
-        columns[None, 3 * D : 4 * D],
-        columns[None, 4 * D : 6 * D],
-        columns[None, 6 * D : 7 * D],
-        columns[None, 7 * D : 7 * D + 8],
-    )
+    rows_of = (3 * D, D, 2 * D, D, 8)
+    results = pl.pallas_call(
+        store_kernel,
+        out_shape=(
+            jax.ShapeDtypeStruct(shape, BF16),
+            jax.ShapeDtypeStruct(shape, BF16),
+            jax.ShapeDtypeStruct(shape, F32),
+            jax.ShapeDtypeStruct(shape, F32),
+        )
+        + tuple(jax.ShapeDtypeStruct((8, rows), F32) for rows in rows_of),
+        in_specs=[anywhere] * 4 + [vmem],
+        out_specs=(anywhere,) * 9,
+        scratch_shapes=[pltpu.VMEM(shape, BF16)] * 2
+        + [pltpu.VMEM(shape, F32)] * 2
+        + [pltpu.VMEM((8, rows), F32) for rows in rows_of]
+        + [pltpu.SemaphoreType.DMA((13,))],
+        name="store",
+    )(node_out, edge_out, node_grad, edge_grad, grads)
+    return results[:4] + tuple(value.T[None] for value in results[4:8]) + (results[8][None],)
 
 
 def solution(mesh):

time: 157 us -> 134 us (0.85)
  local copies, waits for them, and re-layouts: 15.3 us -> 0 us
  Pallas kernels: 140 us -> 132 us
    unnamed x26 -> x0, local copies, waits for them, and re-layouts: 12.7 us -> none
    pallas_call x1, Pallas kernels: 140 us -> 129 us  [local(): pl.pallas_call(kernel, out_shape=(jax.ShapeDtypeStruct(shape, BF16), jax....]
    pallas_call x0 -> x1, Pallas kernels: none -> 3.24 us  [local(): pl.pallas_call(store_kernel, out_shape=(jax.ShapeDtypeStruct(shape, BF16)...]
    broadcast_in_dim x3 -> x0, local copies, waits for them, and re-layouts: 1.85 us -> none  [the longest x1 0.62 us: local(): columns[None, :3 * D]]
where the time goes in v2:
time: 134 us
  Pallas kernels  132 us (99%)
    pallas_call x1, Pallas kernels, local(): pl.pallas_call(kernel, out_shape=(jax.ShapeDtypeStruct(shape, BF16), jax....  129 us
    pallas_call x1, Pallas kernels, local(): pl.pallas_call(store_kernel, out_shape=(jax.ShapeDtypeStruct(shape, BF16)...  3.24 us

profile of v2, /device:TPU:1, one launch (start us, length us, event | category | flops | bytes accessed | tf_op | source)
XLA Modules:
  0.0 133.6 jit_solution(7864585210316736629)
XLA Ops:
  1.3 129.1 %layers.1 = (bf16[1,2,128,512]{3,2,1,0:T(8,128)(2,1)}, bf16[1,2,128,512]{3,2,1,0:T(8,128)(2,1)}, f32[1,2,128,512]{3,2,1,0:T(8,128)}, f32[1,2,128,512]{3,2,1,0:T(8,128)}, f32[2,8,1920]{2,1,0:T(8,128)}) custom-call(bf16[2,128,512]{2,1,0:T(8,128)(2,1)} %node_in.1, bf16[2,128,512]{2,1,0:T(8,128)(2,1)} %edge_in.1, bf16[2,128,512]{2,1,0:T(8,128)(2,1)} %node_cot.1, ...), custom_call_target="tpu_custom_call" | custom-call | tf_op jit(solution)/shard_map/layers/pallas_call | solution.py:790
  130.4 3.2 %store.1 = (bf16[1,2,128,512]{3,2,1,0:T(8,128)(2,1)}, bf16[1,2,128,512]{3,2,1,0:T(8,128)(2,1)}, f32[1,2,128,512]{3,2,1,0:T(8,128)}, f32[1,2,128,512]{3,2,1,0:T(8...) custom-call(bf16[1,2,128,512]{3,2,1,0:T(8,128)(2,1)} %get-tuple-elem, ...), custom_call_target="tpu_custom_call" | custom-call | tf_op jit(solution)/shard_map/store/pallas_call | solution.py:822

commit v3 on v2

--- a/solution.py
+++ b/solution.py
@@ -20,7 +20,7 @@
 DOMS = NY * NZ
 SECTIONS = 4
 HALF = 1920
-LANES_A = 1280
+LANES_A = 1152
 LANES_B = HALF - LANES_A
 CUT_A = 640
 CUT_B = 384
@@ -84,17 +84,12 @@
     vectors,
     coeffs,
     table,
-    edge_x,
-    node_x,
-    snd,
-    rcv,
-    hid_e,
-    pre_e,
+    feats,
+    feats_half,
+    slope_e,
     norm_e,
     scale_e,
-    inc,
-    hid_n,
-    pre_n,
+    slope_n,
     norm_n,
     scale_n,
     node_o,
@@ -109,12 +104,11 @@
     halo_back,
     ret,
     cot_pe,
-    cot_le,
     cot_pn,
-    cot_ln,
+    sender_cot,
+    cot_all,
     vec_acc,
-    grad_half,
-    grad_sib,
+    vec_sib,
     sum_a,
     sum_b,
     half_a,
@@ -149,6 +143,8 @@
     z_peer = [(seg, at * NY + why, core) for at in z_at]
     sibling = (seg, dom, 1 - core)
 
+    edge_x, snd, rcv, hid_e, node_x, inc, hid_n = [feats.at[index] for index in range(7)]
+
     barrier = pltpu.get_barrier_semaphore()
     peers = [
         y_peer[1],
@@ -313,152 +309,82 @@
 
     pl.semaphore_wait(barrier, len(peers))
 
-    def gather(sample):
-        nodes = table[pl.ds(sample * 256, ROWS), :]
-        send_buf[span(sample), :] = dot_nn(send_pick, nodes).astype(BF16)
-        for copy in out_halo(sample):
-            copy.start()
-        node_x[span(sample), :] = nodes
-
-    @pl.when(first)
-    def _():
-        for sample in range(SAMPLES):
-            starts[2 * sample].wait()
-            gather(sample)
-
-    for sample in range(SAMPLES):
+    def lanes_of(side):
+        return pl.ds(pl.multiple_of(side * (D // 2), D // 2), D // 2)
+
+    own_feats = local_copy(
+        feats.at[:, :, lanes_of(core)], feats_half.at[:, pl.ds(0, SAMPLES * ROWS)], 24
+    )
+    pair_feats = remote(
+        feats.at[:, :, lanes_of(1 - core)],
+        feats_half.at[:, pl.ds(SAMPLES * ROWS, SAMPLES * ROWS)],
+        sem_pair,
+        0,
+        sibling,
+    )
+    pair_vec = remote(vec_acc, vec_sib, sem_pair, 4, sibling)
+
+    def pair_cots(sample):
+        return remote(
+            cot_all.at[:, :, pl.ds(sample * ROWS, ROWS)],
+            cot_all.at[:, :, pl.ds((SAMPLES + sample) * ROWS, ROWS)],
+            sem_pair,
+            2 + sample,
+            sibling,
+        )
+
+    def either(at_last, when_last, when_not):
+        if at_last is None:
+            pl.when(last)(when_last)
+            pl.when(jnp.logical_not(last))(when_not)
+        elif at_last:
+            when_last()
+        else:
+            when_not()
+
+    def backward_main(sample, at_last):
         rows = span(sample)
-        if sample == 0:
-
-            @pl.when(jnp.logical_not(first))
-            def _():
-                node_relay(0).wait_recv()
-                gather(0)
-
-            for copy in loads:
-                copy.wait()
-        nodes = node_x[rows, :]
-        receivers = dot_nn(recv_pick, nodes).astype(BF16)
-        rcv[rows, :] = receivers
-        node_part = dot_nn(nodes, w1n[:D, :]) + coeff(4)
-        edge_part = dot_nn(receivers, w1e[2 * D :, :]) + coeff(0)
-
-        @pl.when(first)
-        def _():
-            starts[2 * sample + 1].wait()
-
-        @pl.when(jnp.logical_not(first))
-        def _():
-            edge_relay(sample).wait_recv()
-
-        edges = edge_x[rows, :]
-        edge_part = edge_part + dot_nn(edges, w1e[:D, :])
-        for copy in out_halo(sample):
-            copy.wait_recv()
-        senders = dot_nn(sender_pick, table[pl.ds(sample * 256, 256), :]).astype(BF16)
-        snd[rows, :] = senders
-        edge_pre = edge_part + dot_nn(senders, w1e[D : 2 * D, :])
-        edge_hid = (edge_pre * sigmoid(edge_pre)).astype(BF16)
-        pre_e[rows, :] = edge_pre
-        hid_e[rows, :] = edge_hid
-        edge_norm, edge_scale = norm_parts(dot_nn(edge_hid, w2e[...]) + coeff(1))
-        norm_e[rows, :] = edge_norm
-        scale_e[rows, :] = jnp.broadcast_to(edge_scale, (ROWS, 128))
-        message = (edge_norm * coeff(2) + coeff(3)) * live
-        edge_o[rows, :] = (edges.astype(F32) + message).astype(BF16)
-        if sample == 0:
-
-            @pl.when(jnp.logical_not(last))
-            def _():
-                edge_relay(0).start()
-
-            @pl.when(jnp.logical_not(first))
-            def _():
-                node_relay(1).wait_recv()
-                gather(1)
-
-        incoming = dot_nn(recv_t, message.astype(BF16)).astype(BF16)
-        inc[rows, :] = incoming
-        node_pre = node_part + dot_nn(incoming, w1n[D:, :])
-        node_hid = (node_pre * sigmoid(node_pre)).astype(BF16)
-        pre_n[rows, :] = node_pre
-        hid_n[rows, :] = node_hid
-        node_norm, node_scale = norm_parts(dot_nn(node_hid, w2n[...]) + coeff(5))
-        norm_n[rows, :] = node_norm
-        scale_n[rows, :] = jnp.broadcast_to(node_scale, (ROWS, 128))
-        node_o[rows, :] = (nodes.astype(F32) + node_norm * coeff(6) + coeff(7)).astype(BF16)
-
-        @pl.when(jnp.logical_not(last))
-        def _():
-            node_relay(sample).start()
-            if sample == 1:
-                edge_relay(1).start()
-
-        for copy in outputs(sample):
-            copy.start()
-
-    def silu_slope(values):
-        gate = sigmoid(values)
-        return gate * (1.0 + values * (1.0 - gate))
-
-    for sample in range(SAMPLES):
-        rows = span(sample)
-
-        @pl.when(last)
-        def _():
-            finals[2 * sample].wait()
-
-        @pl.when(jnp.logical_not(last))
-        def _():
-            node_return(sample).wait_recv()
+
+        either(
+            at_last,
+            lambda: finals[2 * sample].wait(),
+            lambda: node_return(sample).wait_recv(),
+        )
 
         node_back = d_node[rows, :].astype(F32)
         node_norm = norm_n[rows, :]
         node_lin_back = norm_back(node_back * coeff(6), node_norm, scale_n[rows, 0:1])
         lin_half = node_lin_back.astype(BF16)
-        cot_ln[rows, :] = lin_half
-        node_pre_back = dot_nt(lin_half, w2n[...]).astype(BF16).astype(F32) * silu_slope(
-            pre_n[rows, :]
-        )
+        node_lin_half = lin_half
+        node_pre_back = dot_nt(lin_half, w2n[...]).astype(BF16).astype(F32) * slope_n[rows, :]
         pre_half = node_pre_back.astype(BF16)
         cot_pn[rows, :] = pre_half
-        node_total = node_back + dot_nt(pre_half, w1n[:D, :]).astype(BF16).astype(F32)
+        node_pre_half = pre_half
         incoming_back = dot_nt(pre_half, w1n[D:, :]).astype(BF16)
 
-        @pl.when(last)
-        def _():
-            finals[2 * sample + 1].wait()
-
-        @pl.when(jnp.logical_not(last))
-        def _():
-            edge_return(sample).wait_recv()
+        either(
+            at_last,
+            lambda: finals[2 * sample + 1].wait(),
+            lambda: edge_return(sample).wait_recv(),
+        )
 
         edge_back = d_edge[rows, :].astype(F32)
         edge_norm = norm_e[rows, :]
         message_back = (edge_back + dot_nn(recv_pick, incoming_back)) * live
         edge_lin_back = norm_back(message_back * coeff(2), edge_norm, scale_e[rows, 0:1])
         lin_half = edge_lin_back.astype(BF16)
-        cot_le[rows, :] = lin_half
-        edge_pre_back = dot_nt(lin_half, w2e[...]).astype(BF16).astype(F32) * silu_slope(
-            pre_e[rows, :]
-        )
+        edge_lin_half = lin_half
+        edge_pre_back = dot_nt(lin_half, w2e[...]).astype(BF16).astype(F32) * slope_e[rows, :]
         pre_half = edge_pre_back.astype(BF16)
         cot_pe[rows, :] = pre_half
         sender_back = dot_nt(pre_half, w1e[D : 2 * D, :]).astype(BF16)
         halo_back[rows, :] = dot_nn(pick_t[ROWS:, :], sender_back).astype(BF16)
         for copy in back_halo(sample):
             copy.start()
-        edge_total = edge_back + dot_nt(pre_half, w1e[:D, :]).astype(BF16).astype(F32)
-        d_edge_f[rows, :] = edge_total
-        d_edge_h[rows, :] = edge_total.astype(BF16)
-
-        @pl.when(jnp.logical_not(first))
-        def _():
-            edge_return(sample).start()
-
-        receiver_back = dot_nt(pre_half, w1e[2 * D :, :]).astype(BF16)
-        node_total = node_total + dot_nn(pick_t[:ROWS, :], sender_back).astype(BF16).astype(F32)
-        node_total = node_total + dot_nn(recv_t, receiver_back).astype(BF16).astype(F32)
+        sender_cot[rows, :] = sender_back
+        for index, value in enumerate((pre_half, edge_lin_half, node_pre_half, node_lin_half)):
+            cot_all[index, :, sample * ROWS : (sample + 1) * ROWS] = value.T
+        pair_cots(sample).start()
         sums = (
             edge_pre_back,
             edge_lin_back,
@@ -471,36 +397,28 @@
         )
         for index, value in enumerate(sums):
             vec_acc[sample, index : index + 1, :] = column_sum(value)
+        if sample == 1:
+            pair_vec.start()
+        edge_total = edge_back + dot_nt(pre_half, w1e[:D, :]).astype(BF16).astype(F32)
+        d_edge_f[rows, :] = edge_total
+        d_edge_h[rows, :] = edge_total.astype(BF16)
+
+        @pl.when(jnp.logical_not(first))
+        def _():
+            edge_return(sample).start()
+
+    def backward_rest(sample):
+        rows = span(sample)
+        node_total = d_node[rows, :].astype(F32)
+        node_total = node_total + dot_nt(cot_pn[rows, :], w1n[:D, :]).astype(BF16).astype(F32)
+        receiver_back = dot_nt(cot_pe[rows, :], w1e[2 * D :, :]).astype(BF16)
+        node_total = node_total + dot_nn(pick_t[:ROWS, :], sender_cot[rows, :]).astype(
+            BF16
+        ).astype(F32)
+        node_total = node_total + dot_nn(recv_t, receiver_back).astype(BF16).astype(F32)
         d_node_f[rows, :] = node_total
 
-    def put(start, value):
-        width = value.shape[1]
-        here = value.astype(BF16)
-        if start >= HALF:
-            grad_half[1, :, start - HALF : start - HALF + width] = here
-        elif start + width <= HALF:
-            grad_half[0, :, start : start + width] = here
-        else:
-            cut = HALF - start
-            grad_half[0, :, start:HALF] = here[:, :cut]
-            grad_half[1, :, 0 : width - cut] = here[:, cut:]
-
-    edge_pre_t = cot_pe[...].T
-    put(0, dot_nn(edge_pre_t, edge_x[...]))
-    put(D, dot_nn(edge_pre_t, snd[...]))
-    put(2 * D, dot_nn(edge_pre_t, rcv[...]))
-    put(3 * D, dot_nn(cot_le[...].T, hid_e[...]))
-    node_pre_t = cot_pn[...].T
-    put(4 * D, dot_nn(node_pre_t, node_x[...]))
-    put(5 * D, dot_nn(node_pre_t, inc[...]))
-    put(6 * D, dot_nn(cot_ln[...].T, hid_n[...]))
-    vec_sum = vec_acc[0] + vec_acc[1]
-    vec_block = jnp.concatenate([vec_sum, jnp.zeros((120, D), F32)], 0).T
-    put(7 * D, jnp.concatenate([vec_block, jnp.zeros((D, 128), F32)], 1))
-
-    pair = remote(grad_half.at[1 - core], grad_sib, sem_pair, 0, sibling)
-    pair.start()
-    for sample in range(SAMPLES):
+    def finish(sample):
         rows = span(sample)
         for copy in back_halo(sample):
             copy.wait_recv()
@@ -515,13 +433,113 @@
         for copy in grad_outputs(sample):
             copy.start()
 
-    pair.wait()
-    for at in range(NZ):
-        here = pl.ds(at * NY * 16, NY * 16)
-        total = grad_half[core, here, :].astype(F32) + grad_sib[here, :].astype(F32)
-        total = total.astype(BF16).reshape(NY, 16, HALF)
-        sum_a[at] = total[:, :, :LANES_A]
-        sum_b[at] = total[:, :, LANES_A:]
+    def gather(sample):
+        nodes = table[pl.ds(sample * 256, ROWS), :]
+        send_buf[span(sample), :] = dot_nn(send_pick, nodes).astype(BF16)
+        for copy in out_halo(sample):
+            copy.start()
+        node_x[span(sample), :] = nodes
+
+    @pl.when(first)
+    def _():
+        for sample in range(SAMPLES):
+            starts[2 * sample].wait()
+            gather(sample)
+
+    for sample in range(SAMPLES):
+        rows = span(sample)
+        if sample == 0:
+
+            @pl.when(jnp.logical_not(first))
+            def _():
+                node_relay(0).wait_recv()
+                gather(0)
+
+            for copy in loads:
+                copy.wait()
+        nodes = node_x[rows, :]
+        receivers = dot_nn(recv_pick, nodes).astype(BF16)
+        rcv[rows, :] = receivers
+        node_part = dot_nn(nodes, w1n[:D, :]) + coeff(4)
+        edge_part = dot_nn(receivers, w1e[2 * D :, :]) + coeff(0)
+
+        @pl.when(first)
+        def _():
+            starts[2 * sample + 1].wait()
+
+        @pl.when(jnp.logical_not(first))
+        def _():
+            edge_relay(sample).wait_recv()
+
+        edges = edge_x[rows, :]
+        edge_part = edge_part + dot_nn(edges, w1e[:D, :])
+        if sample == 0:
+
+            @pl.when(jnp.logical_not(first))
+            def _():
+                node_relay(1).wait_recv()
+                gather(1)
+
+        for copy in out_halo(sample):
+            copy.wait_recv()
+        senders = dot_nn(sender_pick, table[pl.ds(sample * 256, 256), :]).astype(BF16)
+        snd[rows, :] = senders
+        edge_pre = edge_part + dot_nn(senders, w1e[D : 2 * D, :])
+        edge_gate = sigmoid(edge_pre)
+        edge_hid = (edge_pre * edge_gate).astype(BF16)
+        hid_e[rows, :] = edge_hid
+        edge_norm, edge_scale = norm_parts(dot_nn(edge_hid, w2e[...]) + coeff(1))
+        norm_e[rows, :] = edge_norm
+        scale_e[rows, :] = jnp.broadcast_to(edge_scale, (ROWS, 128))
+        message = (edge_norm * coeff(2) + coeff(3)) * live
+        edge_o[rows, :] = (edges.astype(F32) + message).astype(BF16)
+        if sample == 0:
+
+            @pl.when(jnp.logical_not(last))
+            def _():
+                edge_relay(0).start()
+
+        incoming = dot_nn(recv_t, message.astype(BF16)).astype(BF16)
+        inc[rows, :] = incoming
+        node_pre = node_part + dot_nn(incoming, w1n[D:, :])
+        node_gate = sigmoid(node_pre)
+        node_hid = (node_pre * node_gate).astype(BF16)
+        hid_n[rows, :] = node_hid
+        node_norm, node_scale = norm_parts(dot_nn(node_hid, w2n[...]) + coeff(5))
+        norm_n[rows, :] = node_norm
+        scale_n[rows, :] = jnp.broadcast_to(node_scale, (ROWS, 128))
+        node_o[rows, :] = (nodes.astype(F32) + node_norm * coeff(6) + coeff(7)).astype(BF16)
+
+        @pl.when(jnp.logical_not(last))
+        def _():
+            node_relay(sample).start()
+
+        for copy in outputs(sample):
+            copy.start()
+        slope_e[rows, :] = edge_gate * (1.0 + edge_pre * (1.0 - edge_gate))
+        slope_n[rows, :] = node_gate * (1.0 + node_pre * (1.0 - node_gate))
+        if sample == 0:
+
+            @pl.when(last)
+            def _():
+                backward_main(0, True)
+                backward_rest(0)
+
+    @pl.when(jnp.logical_not(last))
+    def _():
+        node_relay(1).wait_send()
+        edge_relay(1).start()
+
+    own_feats.start()
+    pair_feats.start()
+
+    @pl.when(jnp.logical_not(last))
+    def _():
+        backward_main(0, False)
+        backward_rest(0)
+
+    finish(0)
+    backward_main(1, None)
 
     def wide(ref):
         return ref[...].astype(F32)
@@ -619,22 +637,49 @@
     b_y = YFold(
         lambda at, lanes: half_b.at[at, :, lanes], lambda at, lanes: half_b[at, :, lanes], CUT_B, fold_by, 6
     )
-    a_y.start()
-    b_z.start()
+    own_feats.wait()
+    pair_feats.wait_recv()
+    for sample in range(SAMPLES):
+        pair_cots(sample).wait_recv()
+
+    def spread(value):
+        return value.astype(BF16).reshape(NZ, NY, 16, value.shape[1])
+
+    width = D // 2
+    for index, which in enumerate((2, 2, 3)):
+        value = dot_nn(cot_all[which], feats_half[4 + index])
+        sum_b[:, :, :, index * width : (index + 1) * width] = spread(value)
+    pl.when(first)(b_z.start)
+    for index, which in enumerate((0, 0, 0, 1)):
+        value = dot_nn(cot_all[which], feats_half[index])
+        sum_a[:, :, :, index * width : (index + 1) * width] = spread(value)
+    pair_vec.wait_recv()
+    vec_sum = vec_acc[0] + vec_acc[1] + vec_sib[0] + vec_sib[1]
+    vec_block = jnp.concatenate([vec_sum, jnp.zeros((120, D), F32)], 0).T
+    sum_a[:, :, :, 4 * width :] = spread(vec_block)
+    pl.when(first)(a_y.start)
+    backward_rest(1)
+    finish(1)
+
+    @pl.when(jnp.logical_not(first))
+    def _():
+        b_z.start()
+        a_y.start()
+
+    a_y.middle()
     b_z.middle()
-    a_y.middle()
-    half_b[...] = b_z.finish().astype(BF16)
-    b_y.start()
     low, high = a_y.finish()
     half_a[:, :, :CUT_A] = low.astype(BF16)
     half_a[:, :, CUT_A:] = high.astype(BF16)
     a_z.start()
+    half_b[...] = b_z.finish().astype(BF16)
+    b_y.start()
     b_y.middle()
+    a_z.middle()
     low, high = b_y.finish()
     for index, rows in enumerate((slice(0, 8), slice(8, 16))):
         fin[index, :, LANES_A : LANES_A + CUT_B] = low[rows]
         fin[index, :, LANES_A + CUT_B :] = high[rows]
-    a_z.middle()
     total = a_z.finish()
     fin[0, :, :LANES_A] = total[:8]
     fin[1, :, :LANES_A] = total[8:]
@@ -645,6 +690,10 @@
     grads_out[1 - core] = fin_sib[...]
 
     swap.wait_send()
+    pair_feats.wait_send()
+    pair_vec.wait_send()
+    for sample in range(SAMPLES):
+        pair_cots(sample).wait_send()
     for copy in a_y.all + b_z.all + a_z.all + b_y.all:
         copy.wait_send()
     for sample in range(SAMPLES):
@@ -656,7 +705,8 @@
         @pl.when(jnp.logical_not(last))
         def _():
             edge_relay(sample).wait_send()
-            node_relay(sample).wait_send()
+            if sample == 0:
+                node_relay(0).wait_send()
 
         @pl.when(jnp.logical_not(first))
         def _():
@@ -664,8 +714,10 @@
             node_return(sample).wait_send()
 
 
-def store_kernel(node_out, edge_out, node_grad, edge_grad, grads, *refs):
-    results, held, rows_held, sems = refs[:9], refs[9:13], refs[13:18], refs[18]
+def store_kernel(node_out, edge_out, node_grad, edge_grad, grads_hbm, *refs):
+    results, held, rows_held, grads, sems = refs[:9], refs[9:13], refs[13:18], refs[18], refs[19]
+    grads_load = pltpu.make_async_copy(grads_hbm, grads, sems.at[13])
+    grads_load.start()
     sources = (node_out, edge_out, node_grad, edge_grad)
     loads = [
         pltpu.make_async_copy(source, target, sems.at[index])
@@ -678,12 +730,17 @@
     for copy in loads:
         copy.start()
     w1e_rows, w2e_rows, w1n_rows, w2n_rows, vec_rows = rows_held
-    w1e_rows[:, :] = grads[0, :, : 3 * D]
-    w2e_rows[:, : HALF - 3 * D] = grads[0, :, 3 * D :]
-    w2e_rows[:, HALF - 3 * D :] = grads[1, :, : 4 * D - HALF]
-    w1n_rows[:, :] = grads[1, :, 4 * D - HALF : 6 * D - HALF]
-    w2n_rows[:, :] = grads[1, :, 6 * D - HALF : 7 * D - HALF]
-    columns = grads[1, :, 7 * D - HALF : 7 * D - HALF + 128].T
+    grads_load.wait()
+    width = D // 2
+    places = [(w1e_rows, 0), (w1e_rows, D), (w1e_rows, 2 * D), (w2e_rows, 0)]
+    places += [(w1n_rows, 0), (w1n_rows, D), (w2n_rows, 0)]
+    for index, (target, start) in enumerate(places):
+        lane = index * width if index < 4 else LANES_A + (index - 4) * width
+        for side in range(2):
+            target[:, start + side * width : start + (side + 1) * width] = grads[
+                side, :, lane : lane + width
+            ]
+    columns = grads[0, :, 4 * width : 4 * width + 128].T
     vec_rows[...] = columns[:8, :]
     for copy in stores[4:]:
         copy.start()
@@ -738,16 +795,11 @@
         half(8, D),
         full(8, D),
         half(2 * both, D),
-        half(both, D),
-        half(both, D),
-        half(both, D),
-        half(both, D),
-        half(both, D),
+        half(7, both, D),
+        half(7, 2 * both, D // 2),
         full(both, D),
         full(both, D),
         full(both, 128),
-        half(both, D),
-        half(both, D),
         full(both, D),
         full(both, D),
         full(both, 128),
@@ -765,10 +817,9 @@
         half(both, D),
         half(both, D),
         half(both, D),
-        half(both, D),
+        half(4, D, 2 * both),
         full(SAMPLES, 8, D),
-        half(2, D, HALF),
-        half(D, HALF),
+        full(SAMPLES, 8, D),
         half(NZ, NY, 16, LANES_A),
         half(NZ, NY, 16, LANES_B),
         half(NZ, 16, LANES_A),
@@ -779,10 +830,10 @@
         y_parts((16,), LANES_B, CUT_B),
         full(2, 8, HALF),
         full(8, HALF),
-        pltpu.SemaphoreType.DMA((24,)),
+        pltpu.SemaphoreType.DMA((25,)),
         pltpu.SemaphoreType.DMA((2, 8)),
         pltpu.SemaphoreType.DMA((2, 8)),
-        pltpu.SemaphoreType.DMA((2, 2)),
+        pltpu.SemaphoreType.DMA((2, 5)),
         pltpu.SemaphoreType.DMA((2, 12)),
         pltpu.SemaphoreType.DMA((2, 16)),
     ]
@@ -828,12 +879,12 @@
             jax.ShapeDtypeStruct(shape, F32),
         )
         + tuple(jax.ShapeDtypeStruct((8, rows), F32) for rows in rows_of),
-        in_specs=[anywhere] * 4 + [vmem],
+        in_specs=[anywhere] * 5,
         out_specs=(anywhere,) * 9,
         scratch_shapes=[pltpu.VMEM(shape, BF16)] * 2
         + [pltpu.VMEM(shape, F32)] * 2
         + [pltpu.VMEM((8, rows), F32) for rows in rows_of]
-        + [pltpu.SemaphoreType.DMA((13,))],
+        + [pltpu.VMEM((2, 8, HALF), F32), pltpu.SemaphoreType.DMA((14,))],
         name="store",
     )(node_out, edge_out, node_grad, edge_grad, grads)
     return results[:4] + tuple(value.T[None] for value in results[4:8]) + (results[8][None],)

time: 134 us -> 125 us (0.933)
  Pallas kernels: 132 us -> 123 us
    pallas_call x1, Pallas kernels: 129 us -> 121 us  [local(): pl.pallas_call(kernel, out_shape=(jax.ShapeDtypeStruct(shape, BF16), jax....]
where the time goes in v3:
time: 125 us
  Pallas kernels  123 us (98%)
  between operations  1.3 us (1%)
    pallas_call x1, Pallas kernels, local(): pl.pallas_call(kernel, out_shape=(jax.ShapeDtypeStruct(shape, BF16), jax....  121 us

profile of v3, /device:TPU:1, one launch (start us, length us, event | category | flops | bytes accessed | tf_op | source)
XLA Modules:
  0.0 124.5 jit_solution(16145499742539282754)
XLA Ops:
  1.3 120.8 %layers.1 = (bf16[1,2,128,512]{3,2,1,0:T(8,128)(2,1)}, bf16[1,2,128,512]{3,2,1,0:T(8,128)(2,1)}, f32[1,2,128,512]{3,2,1,0:T(8,128)}, f32[1,2,128,512]{3,2,1,0:T(8,128)}, f32[2,8,1920]{2,1,0:T(8,128)}) custom-call(bf16[2,128,512]{2,1,0:T(8,128)(2,1)} %node_in.1, bf16[2,128,512]{2,1,0:T(8,128)(2,1)} %edge_in.1, bf16[2,128,512]{2,1,0:T(8,128)(2,1)} %node_cot.1, ...), custom_call_target="tpu_custom_call" | custom-call | tf_op jit(solution)/shard_map/layers/pallas_call | solution.py:841
  122.1 2.4 %store.1 = (bf16[1,2,128,512]{3,2,1,0:T(8,128)(2,1)}, bf16[1,2,128,512]{3,2,1,0:T(8,128)(2,1)}, f32[1,2,128,512]{3,2,1,0:T(8,128)}, f32[1,2,128,512]{3,2,1,0:T(8...) custom-call(bf16[1,2,128,512]{3,2,1,0:T(8,128)(2,1)} %get-tuple-elem, ...), custom_call_target="tpu_custom_call" | custom-call | tf_op jit(solution)/shard_map/store/pallas_call | solution.py:873

commit v4 on v3

--- a/solution.py
+++ b/solution.py
@@ -20,9 +20,11 @@
 DOMS = NY * NZ
 SECTIONS = 4
 HALF = 1920
-LANES_A = 1152
-LANES_B = HALF - LANES_A
-CUT_A = 640
+LANES_A = 512
+LANES_V = 640
+LANES_B = HALF - LANES_A - LANES_V
+CUT_A = 256
+CUT_V = 384
 CUT_B = 384
 
 
@@ -110,13 +112,17 @@
     vec_acc,
     vec_sib,
     sum_a,
+    sum_v,
     sum_b,
     half_a,
+    half_v,
     half_b,
     fold_ay,
+    fold_vy,
     fold_bz,
     fold_az,
-    fold_by,
+    fold_vz,
+    recv_by,
     fin,
     fin_sib,
     sem_local,
@@ -148,6 +154,7 @@
     barrier = pltpu.get_barrier_semaphore()
     peers = [
         y_peer[1],
+        y_peer[2],
         y_peer[3],
         z_peer[1],
         z_peer[2],
@@ -322,14 +329,14 @@
         0,
         sibling,
     )
-    pair_vec = remote(vec_acc, vec_sib, sem_pair, 4, sibling)
-
-    def pair_cots(sample):
+    pair_vec = remote(vec_acc, vec_sib, sem_pair, 2, sibling)
+
+    def pair_cots(sample, part):
         return remote(
-            cot_all.at[:, :, pl.ds(sample * ROWS, ROWS)],
-            cot_all.at[:, :, pl.ds((SAMPLES + sample) * ROWS, ROWS)],
+            cot_all.at[pl.ds(2 * part, 2), :, pl.ds(sample * ROWS, ROWS)],
+            cot_all.at[pl.ds(2 * part, 2), :, pl.ds((SAMPLES + sample) * ROWS, ROWS)],
             sem_pair,
-            2 + sample,
+            3 + 2 * sample + part,
             sibling,
         )
 
@@ -361,6 +368,9 @@
         cot_pn[rows, :] = pre_half
         node_pre_half = pre_half
         incoming_back = dot_nt(pre_half, w1n[D:, :]).astype(BF16)
+        for index, value in enumerate((node_pre_half, node_lin_half)):
+            cot_all[2 + index, :, sample * ROWS : (sample + 1) * ROWS] = value.T
+        pair_cots(sample, 1).start()
 
         either(
             at_last,
@@ -382,9 +392,9 @@
         for copy in back_halo(sample):
             copy.start()
         sender_cot[rows, :] = sender_back
-        for index, value in enumerate((pre_half, edge_lin_half, node_pre_half, node_lin_half)):
+        for index, value in enumerate((pre_half, edge_lin_half)):
             cot_all[index, :, sample * ROWS : (sample + 1) * ROWS] = value.T
-        pair_cots(sample).start()
+        pair_cots(sample, 0).start()
         sums = (
             edge_pre_back,
             edge_lin_back,
@@ -629,18 +639,28 @@
             total = self.source[z_at[0]].astype(F32) + wide(self.r1p) + wide(self.r1m)
             return total + wide(self.r2p) + wide(self.r2m)
 
-    a_y = YFold(
-        lambda at, lanes: sum_a.at[:, at, :, lanes], lambda at, lanes: sum_a[:, at, :, lanes], CUT_A, fold_ay, 0
-    )
+    def folds(source, half, y_bufs, z_bufs, cut, y_base, z_base):
+        y_fold = YFold(
+            lambda at, lanes: source.at[:, at, :, lanes],
+            lambda at, lanes: source[:, at, :, lanes],
+            cut,
+            y_bufs,
+            y_base,
+        )
+        return y_fold, ZFold(half, cut, z_bufs, z_base)
+
+    a_y, a_z = folds(sum_a, half_a, fold_ay, fold_az, CUT_A, 0, 8)
+    v_y, v_z = folds(sum_v, half_v, fold_vy, fold_vz, CUT_V, 6, 16)
     b_z = ZFold(sum_b, CUT_B, fold_bz, 0)
-    a_z = ZFold(half_a, CUT_A, fold_az, 8)
-    b_y = YFold(
-        lambda at, lanes: half_b.at[at, :, lanes], lambda at, lanes: half_b[at, :, lanes], CUT_B, fold_by, 6
-    )
+    b_y = [
+        remote(half_b.at[y_at[k]], recv_by.at[k - 1], sem_y, 11 + k, y_peer[k])
+        for k in range(1, NY)
+    ]
+
     own_feats.wait()
     pair_feats.wait_recv()
     for sample in range(SAMPLES):
-        pair_cots(sample).wait_recv()
+        pair_cots(sample, 1).wait_recv()
 
     def spread(value):
         return value.astype(BF16).reshape(NZ, NY, 16, value.shape[1])
@@ -650,14 +670,20 @@
         value = dot_nn(cot_all[which], feats_half[4 + index])
         sum_b[:, :, :, index * width : (index + 1) * width] = spread(value)
     pl.when(first)(b_z.start)
-    for index, which in enumerate((0, 0, 0, 1)):
-        value = dot_nn(cot_all[which], feats_half[index])
+    for sample in range(SAMPLES):
+        pair_cots(sample, 0).wait_recv()
+    for index in range(2):
+        value = dot_nn(cot_all[0], feats_half[index])
         sum_a[:, :, :, index * width : (index + 1) * width] = spread(value)
+    pl.when(first)(a_y.start)
+    for index, which in enumerate((0, 1)):
+        value = dot_nn(cot_all[which], feats_half[2 + index])
+        sum_v[:, :, :, index * width : (index + 1) * width] = spread(value)
     pair_vec.wait_recv()
     vec_sum = vec_acc[0] + vec_acc[1] + vec_sib[0] + vec_sib[1]
     vec_block = jnp.concatenate([vec_sum, jnp.zeros((120, D), F32)], 0).T
-    sum_a[:, :, :, 4 * width :] = spread(vec_block)
-    pl.when(first)(a_y.start)
+    sum_v[:, :, :, 2 * width :] = spread(vec_block)
+    pl.when(first)(v_y.start)
     backward_rest(1)
     finish(1)
 
@@ -665,24 +691,35 @@
     def _():
         b_z.start()
         a_y.start()
+        v_y.start()
+
+    def joined(parts):
+        return jnp.concatenate(parts, -1)
+
+    def keep(value, start):
+        lanes = slice(start, start + value.shape[1])
+        fin[0, :, lanes] = value[:8]
+        fin[1, :, lanes] = value[8:]
 
     a_y.middle()
     b_z.middle()
-    low, high = a_y.finish()
-    half_a[:, :, :CUT_A] = low.astype(BF16)
-    half_a[:, :, CUT_A:] = high.astype(BF16)
+    v_y.middle()
+    half_a[...] = joined(a_y.finish()).astype(BF16)
     a_z.start()
+    half_v[...] = joined(v_y.finish()).astype(BF16)
+    v_z.start()
     half_b[...] = b_z.finish().astype(BF16)
-    b_y.start()
-    b_y.middle()
+    for copy in b_y:
+        copy.start()
     a_z.middle()
-    low, high = b_y.finish()
-    for index, rows in enumerate((slice(0, 8), slice(8, 16))):
-        fin[index, :, LANES_A : LANES_A + CUT_B] = low[rows]
-        fin[index, :, LANES_A + CUT_B :] = high[rows]
-    total = a_z.finish()
-    fin[0, :, :LANES_A] = total[:8]
-    fin[1, :, :LANES_A] = total[8:]
+    v_z.middle()
+    total = half_b[y_at[0]].astype(F32)
+    for index, copy in enumerate(b_y):
+        copy.wait_recv()
+        total = total + recv_by[index].astype(F32)
+    keep(total, LANES_A + LANES_V)
+    keep(a_z.finish(), 0)
+    keep(v_z.finish(), LANES_A)
     swap = remote(fin.at[1 - core], fin_sib, sem_pair, 1, sibling)
     swap.start()
     swap.wait_recv()
@@ -693,8 +730,9 @@
     pair_feats.wait_send()
     pair_vec.wait_send()
     for sample in range(SAMPLES):
-        pair_cots(sample).wait_send()
-    for copy in a_y.all + b_z.all + a_z.all + b_y.all:
+        pair_cots(sample, 0).wait_send()
+        pair_cots(sample, 1).wait_send()
+    for copy in (*a_y.all, *b_z.all, *a_z.all, *v_y.all, *v_z.all, *b_y):
         copy.wait_send()
     for sample in range(SAMPLES):
         for copy in out_halo(sample) + back_halo(sample):
@@ -735,7 +773,7 @@
     places = [(w1e_rows, 0), (w1e_rows, D), (w1e_rows, 2 * D), (w2e_rows, 0)]
     places += [(w1n_rows, 0), (w1n_rows, D), (w2n_rows, 0)]
     for index, (target, start) in enumerate(places):
-        lane = index * width if index < 4 else LANES_A + (index - 4) * width
+        lane = index * width if index < 4 else HALF - LANES_B + (index - 4) * width
         for side in range(2):
             target[:, start + side * width : start + (side + 1) * width] = grads[
                 side, :, lane : lane + width
@@ -821,21 +859,25 @@
         full(SAMPLES, 8, D),
         full(SAMPLES, 8, D),
         half(NZ, NY, 16, LANES_A),
+        half(NZ, NY, 16, LANES_V),
         half(NZ, NY, 16, LANES_B),
         half(NZ, 16, LANES_A),
+        half(NZ, 16, LANES_V),
         half(NY, 16, LANES_B),
         y_parts((NZ, 16), LANES_A, CUT_A),
+        y_parts((NZ, 16), LANES_V, CUT_V),
         z_parts((NY, 16), LANES_B, CUT_B),
         z_parts((16,), LANES_A, CUT_A),
-        y_parts((16,), LANES_B, CUT_B),
+        z_parts((16,), LANES_V, CUT_V),
+        half(NY - 1, 16, LANES_B),
         full(2, 8, HALF),
         full(8, HALF),
         pltpu.SemaphoreType.DMA((25,)),
         pltpu.SemaphoreType.DMA((2, 8)),
         pltpu.SemaphoreType.DMA((2, 8)),
-        pltpu.SemaphoreType.DMA((2, 5)),
-        pltpu.SemaphoreType.DMA((2, 12)),
-        pltpu.SemaphoreType.DMA((2, 16)),
+        pltpu.SemaphoreType.DMA((2, 7)),
+        pltpu.SemaphoreType.DMA((2, 15)),
+        pltpu.SemaphoreType.DMA((2, 24)),
     ]
     shape = (1, SAMPLES, ROWS, D)
     node_out, edge_out, node_grad, edge_grad, grads = pl.pallas_call(

time: 125 us -> 122 us (0.976)
  Pallas kernels: 123 us -> 121 us
    pallas_call x1, Pallas kernels: 121 us -> 118 us  [local(): pl.pallas_call(kernel, out_shape=(jax.ShapeDtypeStruct(shape, BF16), jax....]
where the time goes in v4:
time: 122 us
  Pallas kernels  121 us (99%)
  between operations  1.3 us (1%)
    pallas_call x1, Pallas kernels, local(): pl.pallas_call(kernel, out_shape=(jax.ShapeDtypeStruct(shape, BF16), jax....  118 us

profile of v4, /device:TPU:1, one launch (start us, length us, event | category | flops | bytes accessed | tf_op | source)
XLA Modules:
  0.0 121.9 jit_solution(5142153436659589226)
XLA Ops:
  1.3 118.2 %layers.1 = (bf16[1,2,128,512]{3,2,1,0:T(8,128)(2,1)}, bf16[1,2,128,512]{3,2,1,0:T(8,128)(2,1)}, f32[1,2,128,512]{3,2,1,0:T(8,128)}, f32[1,2,128,512]{3,2,1,0:T(8,128)}, f32[2,8,1920]{2,1,0:T(8,128)}) custom-call(bf16[2,128,512]{2,1,0:T(8,128)(2,1)} %node_in.1, bf16[2,128,512]{2,1,0:T(8,128)(2,1)} %edge_in.1, bf16[2,128,512]{2,1,0:T(8,128)(2,1)} %node_cot.1, ...), custom_call_target="tpu_custom_call" | custom-call | tf_op jit(solution)/shard_map/layers/pallas_call | solution.py:883
  119.5 2.4 %store.1 = (bf16[1,2,128,512]{3,2,1,0:T(8,128)(2,1)}, bf16[1,2,128,512]{3,2,1,0:T(8,128)(2,1)}, f32[1,2,128,512]{3,2,1,0:T(8,128)}, f32[1,2,128,512]{3,2,1,0:T(8...) custom-call(bf16[1,2,128,512]{3,2,1,0:T(8,128)(2,1)} %get-tuple-elem, ...), custom_call_target="tpu_custom_call" | custom-call | tf_op jit(solution)/shard_map/store/pallas_call | solution.py:915

commit v5 on v4

--- a/solution.py
+++ b/solution.py
@@ -242,36 +242,41 @@
             device_id_type=MESH,
         )
 
-    def halo_copies(source, sample, target_ref, base, kind):
+    def part_of(part):
+        return pl.ds(part * (D // 2), D // 2)
+
+    def halo_copies(source, sample, part, target_ref, base, kind):
+        index = kind * 8 + sample * 4 + part * 2
+        lanes = part_of(part)
         return (
             remote(
-                source.at[pl.ds(sample * ROWS, HALO)],
-                target_ref.at[pl.ds(base + HALO, HALO)],
+                source.at[pl.ds(sample * ROWS, HALO), lanes],
+                target_ref.at[pl.ds(base + HALO, HALO), lanes],
                 sem_halo,
-                kind * 4 + sample * 2,
+                index,
                 (seg, dom_prev, core),
             ),
             remote(
-                source.at[pl.ds(sample * ROWS + HALO, HALO)],
-                target_ref.at[pl.ds(base, HALO)],
+                source.at[pl.ds(sample * ROWS + HALO, HALO), lanes],
+                target_ref.at[pl.ds(base, HALO), lanes],
                 sem_halo,
-                kind * 4 + sample * 2 + 1,
+                index + 1,
                 (seg, dom_next, core),
             ),
         )
 
-    def out_halo(sample):
-        return halo_copies(send_buf, sample, table, sample * 256 + ROWS, 0)
-
-    def back_halo(sample):
-        return halo_copies(halo_back, sample, ret, sample * ROWS, 1)
-
-    def node_relay(sample):
+    def out_halo(sample, part):
+        return halo_copies(send_buf, sample, part, table, sample * 256 + ROWS, 0)
+
+    def back_halo(sample, part):
+        return halo_copies(halo_back, sample, part, ret, sample * ROWS, 1)
+
+    def node_relay(sample, part):
         return remote(
-            node_o.at[span(sample)],
-            table.at[pl.ds(sample * 256, ROWS)],
+            node_o.at[span(sample), part_of(part)],
+            table.at[pl.ds(sample * 256, ROWS), part_of(part)],
             sem_relay,
-            sample,
+            sample * 2 + part,
             (ahead, dom, core),
         )
 
@@ -280,16 +285,16 @@
             edge_o.at[span(sample)],
             edge_x.at[span(sample)],
             sem_relay,
-            2 + sample,
+            4 + sample,
             (ahead, dom, core),
         )
 
-    def node_return(sample):
+    def node_return(sample, part):
         return remote(
-            d_node_h.at[span(sample)],
-            d_node.at[span(sample)],
+            d_node_h.at[span(sample), part_of(part)],
+            d_node.at[span(sample), part_of(part)],
             sem_relay,
-            4 + sample,
+            6 + sample * 2 + part,
             (behind, dom, core),
         )
 
@@ -298,7 +303,7 @@
             d_edge_h.at[span(sample)],
             d_edge.at[span(sample)],
             sem_relay,
-            6 + sample,
+            10 + sample,
             (behind, dom, core),
         )
 
@@ -355,7 +360,7 @@
         either(
             at_last,
             lambda: finals[2 * sample].wait(),
-            lambda: node_return(sample).wait_recv(),
+            lambda: [node_return(sample, part).wait_recv() for part in range(2)] and None,
         )
 
         node_back = d_node[rows, :].astype(F32)
@@ -387,11 +392,15 @@
         edge_pre_back = dot_nt(lin_half, w2e[...]).astype(BF16).astype(F32) * slope_e[rows, :]
         pre_half = edge_pre_back.astype(BF16)
         cot_pe[rows, :] = pre_half
-        sender_back = dot_nt(pre_half, w1e[D : 2 * D, :]).astype(BF16)
-        halo_back[rows, :] = dot_nn(pick_t[ROWS:, :], sender_back).astype(BF16)
-        for copy in back_halo(sample):
-            copy.start()
-        sender_cot[rows, :] = sender_back
+        for part in range(2):
+            lanes = slice(part * (D // 2), (part + 1) * (D // 2))
+            sender_back = dot_nt(
+                pre_half, w1e[D + part * (D // 2) : D + (part + 1) * (D // 2), :]
+            ).astype(BF16)
+            halo_back[rows, lanes] = dot_nn(pick_t[ROWS:, :], sender_back).astype(BF16)
+            for copy in back_halo(sample, part):
+                copy.start()
+            sender_cot[rows, lanes] = sender_back
         for index, value in enumerate((pre_half, edge_lin_half)):
             cot_all[index, :, sample * ROWS : (sample + 1) * ROWS] = value.T
         pair_cots(sample, 0).start()
@@ -430,31 +439,34 @@
 
     def finish(sample):
         rows = span(sample)
-        for copy in back_halo(sample):
-            copy.wait_recv()
-        node_total = d_node_f[rows, :] + dot_nn(send_t, ret[rows, :])
-        d_node_f[rows, :] = node_total
-        d_node_h[rows, :] = node_total.astype(BF16)
-
-        @pl.when(jnp.logical_not(first))
-        def _():
-            node_return(sample).start()
+        for part in range(2):
+            lanes = slice(part * (D // 2), (part + 1) * (D // 2))
+            for copy in back_halo(sample, part):
+                copy.wait_recv()
+            node_total = d_node_f[rows, lanes] + dot_nn(send_t, ret[rows, lanes])
+            d_node_f[rows, lanes] = node_total
+            d_node_h[rows, lanes] = node_total.astype(BF16)
+            pl.when(jnp.logical_not(first))(node_return(sample, part).start)
 
         for copy in grad_outputs(sample):
             copy.start()
 
-    def gather(sample):
-        nodes = table[pl.ds(sample * 256, ROWS), :]
-        send_buf[span(sample), :] = dot_nn(send_pick, nodes).astype(BF16)
-        for copy in out_halo(sample):
-            copy.start()
-        node_x[span(sample), :] = nodes
+    def gather(sample, relayed):
+        for part in range(2):
+            lanes = slice(part * (D // 2), (part + 1) * (D // 2))
+            if relayed:
+                node_relay(sample, part).wait_recv()
+            nodes = table[pl.ds(sample * 256, ROWS), lanes]
+            send_buf[span(sample), lanes] = dot_nn(send_pick, nodes).astype(BF16)
+            for copy in out_halo(sample, part):
+                copy.start()
+            node_x[span(sample), lanes] = nodes
 
     @pl.when(first)
     def _():
         for sample in range(SAMPLES):
             starts[2 * sample].wait()
-            gather(sample)
+            gather(sample, False)
 
     for sample in range(SAMPLES):
         rows = span(sample)
@@ -462,8 +474,7 @@
 
             @pl.when(jnp.logical_not(first))
             def _():
-                node_relay(0).wait_recv()
-                gather(0)
+                gather(0, True)
 
             for copy in loads:
                 copy.wait()
@@ -487,11 +498,11 @@
 
             @pl.when(jnp.logical_not(first))
             def _():
-                node_relay(1).wait_recv()
-                gather(1)
-
-        for copy in out_halo(sample):
-            copy.wait_recv()
+                gather(1, True)
+
+        for part in range(2):
+            for copy in out_halo(sample, part):
+                copy.wait_recv()
         senders = dot_nn(sender_pick, table[pl.ds(sample * 256, 256), :]).astype(BF16)
         snd[rows, :] = senders
         edge_pre = edge_part + dot_nn(senders, w1e[D : 2 * D, :])
@@ -522,7 +533,8 @@
 
         @pl.when(jnp.logical_not(last))
         def _():
-            node_relay(sample).start()
+            for part in range(2):
+                node_relay(sample, part).start()
 
         for copy in outputs(sample):
             copy.start()
@@ -537,7 +549,8 @@
 
     @pl.when(jnp.logical_not(last))
     def _():
-        node_relay(1).wait_send()
+        for part in range(2):
+            node_relay(1, part).wait_send()
         edge_relay(1).start()
 
     own_feats.start()
@@ -735,8 +748,9 @@
     for copy in (*a_y.all, *b_z.all, *a_z.all, *v_y.all, *v_z.all, *b_y):
         copy.wait_send()
     for sample in range(SAMPLES):
-        for copy in out_halo(sample) + back_halo(sample):
-            copy.wait_send()
+        for part in range(2):
+            for copy in out_halo(sample, part) + back_halo(sample, part):
+                copy.wait_send()
         for copy in outputs(sample) + grad_outputs(sample):
             copy.wait()
 
@@ -744,12 +758,14 @@
         def _():
             edge_relay(sample).wait_send()
             if sample == 0:
-                node_relay(0).wait_send()
+                for part in range(2):
+                    node_relay(0, part).wait_send()
 
         @pl.when(jnp.logical_not(first))
         def _():
             edge_return(sample).wait_send()
-            node_return(sample).wait_send()
+            for part in range(2):
+                node_return(sample, part).wait_send()
 
 
 def store_kernel(node_out, edge_out, node_grad, edge_grad, grads_hbm, *refs):
@@ -873,8 +889,8 @@
         full(2, 8, HALF),
         full(8, HALF),
         pltpu.SemaphoreType.DMA((25,)),
-        pltpu.SemaphoreType.DMA((2, 8)),
-        pltpu.SemaphoreType.DMA((2, 8)),
+        pltpu.SemaphoreType.DMA((2, 12)),
+        pltpu.SemaphoreType.DMA((2, 16)),
         pltpu.SemaphoreType.DMA((2, 7)),
         pltpu.SemaphoreType.DMA((2, 15)),
         pltpu.SemaphoreType.DMA((2, 24)),

time: 122 us -> 121 us (level)
  no operation moved by 1% of the time
where the time goes in v5:
time: 121 us
  Pallas kernels  120 us (99%)
  between operations  1.3 us (1%)
    pallas_call x1, Pallas kernels, local(): pl.pallas_call(kernel, out_shape=(jax.ShapeDtypeStruct(shape, BF16), jax....  118 us

profile of v5, /device:TPU:1, one launch (start us, length us, event | category | flops | bytes accessed | tf_op | source)
XLA Modules:
  0.0 121.3 jit_solution(9677169200645316006)
XLA Ops:
  1.3 117.6 %layers.1 = (bf16[1,2,128,512]{3,2,1,0:T(8,128)(2,1)}, bf16[1,2,128,512]{3,2,1,0:T(8,128)(2,1)}, f32[1,2,128,512]{3,2,1,0:T(8,128)}, f32[1,2,128,512]{3,2,1,0:T(8,128)}, f32[2,8,1920]{2,1,0:T(8,128)}) custom-call(bf16[2,128,512]{2,1,0:T(8,128)(2,1)} %node_in.1, bf16[2,128,512]{2,1,0:T(8,128)(2,1)} %edge_in.1, bf16[2,128,512]{2,1,0:T(8,128)(2,1)} %node_cot.1, ...), custom_call_target="tpu_custom_call" | custom-call | tf_op jit(solution)/shard_map/layers/pallas_call | solution.py:899
  118.9 2.4 %store.1 = (bf16[1,2,128,512]{3,2,1,0:T(8,128)(2,1)}, bf16[1,2,128,512]{3,2,1,0:T(8,128)(2,1)}, f32[1,2,128,512]{3,2,1,0:T(8,128)}, f32[1,2,128,512]{3,2,1,0:T(8...) custom-call(bf16[1,2,128,512]{3,2,1,0:T(8,128)(2,1)} %get-tuple-elem, ...), custom_call_target="tpu_custom_call" | custom-call | tf_op jit(solution)/shard_map/store/pallas_call | solution.py:931
